TPU v7x, 256 devices: a whole 4x4x8 slice. The times are simulated.
256 devices in a mesh: agent: 32 (over y, x, core), env: 8 (over z).
Axes of the slice: x: 4, y: 4, z: 8, core: 2. Of those that a mesh axis runs over, the one named last changes fastest.
Arguments:
- obs_rep: bfloat16 [8, 8192, 1024], P('env', 'agent'), may hold values from -6 to 6
- actions: int32 [8, 8192], P('env', 'agent'), may hold values from 0 to 31
- action_table: bfloat16 [32, 1024], replicated, may hold values from -6 to 6
- decode_rank: int32 [64], replicated, may hold values from 0 to 63, each once
- visible: int32 [64, 64], replicated, may hold values 0 or 1
- w_query: bfloat16 [1024, 1024], replicated, may hold values from -1 to 1
- w_key: bfloat16 [1024, 1024], replicated, may hold values from -1 to 1
- w_value: bfloat16 [1024, 1024], replicated, may hold values from -0.1875 to 0.1875
- w_out: bfloat16 [1024, 1024], replicated, may hold values from -0.1875 to 0.1875
- norm_gain: float32 [1024], replicated, may hold values from 0.5 to 1.5
- w_mix: bfloat16 [1024, 512], replicated, may hold values from -0.1875 to 0.1875
- w_group: bfloat16 [1024, 512], replicated, may hold values from -0.1875 to 0.1875
- w_head: float32 [512], replicated, may hold values from -0.25 to 0.25
- returns: float32 [8, 8192], P(None, ('agent', 'env')), may hold values from -6 to 6
- group_of_env: int32 [8], replicated, may hold values from 0 to 3, as said below
Outputs:
- value: float32 [8, 8192], P(None, ('agent', 'env'))
- advantage: float32 [8, 8192], P(None, ('agent', 'env'))
Inputs may be any that keep to these rules, and one draw needn't show every extreme that they name: `group_of_env`: each group number names exactly 2 environments. `decode_rank`: each block's position occurs once.
All inputs are finite; a program needn't handle non-finite values.
Results may differ from a plain program's by a relative error of at most 0.01.
Values may be sent and summed in bfloat16 or wider, within the bound.
A program may use at most 384 MiB of HBM per device.

v0:
```python
import functools

import jax
import jax.numpy as jnp
import numpy as np
from jax import lax
from jax.experimental import pallas as pl
from jax.experimental.pallas import tpu as pltpu
from jax.sharding import PartitionSpec as P

H = 16
BLK = 128
HALF = BLK // 2
HD = 64
LOG2E = 1.4426950408889634
NEG = -1e30
VROWS = 80
QN = 256
SIDE = 4
MESH = pl.DeviceIdType.MESH
BF = jnp.bfloat16
F32 = jnp.float32


def agent_at(y, x, core):
    return (y * SIDE + x) * 2 + core


def greet_plane(me):
    barrier = pltpu.get_barrier_semaphore()

    def tell(step, _):
        other = lax.rem(me + step, 2 * SIDE * SIDE)
        pl.semaphore_signal(barrier, inc=1, device_id={"agent": other}, device_id_type=MESH)
        return 0

    lax.fori_loop(1, 2 * SIDE * SIDE, tell, 0)
    return barrier


def project_kernel(
    obs_ref, act_ref, table_ref, wq_hbm, wk_hbm, wv_hbm,
    qbuf, kbuf, vbuf,
    wq, wk, wv, tok, kst, vst, qst, load_sem,
    ks_send, ks_recv, vs_send, vs_recv, qs_send, qs_recv, kf_send, kf_recv, vf_send, vf_recv, local_sem,
):
    me = lax.axis_index("agent")
    core = lax.rem(me, 2)
    chip = me // 2
    my_y, my_x = chip // SIDE, lax.rem(chip, SIDE)
    chips = SIDE * SIDE
    sibling = chip * 2 + 1 - core
    loads = [
        pltpu.make_async_copy(src, dst, load_sem.at[n])
        for n, (src, dst) in enumerate(((wk_hbm, wk), (wv_hbm, wv), (wq_hbm, wq)))
    ]
    for load in loads:
        load.start()
    barrier = greet_plane(me)

    onehot = (act_ref[...] == lax.broadcasted_iota(jnp.int32, (table_ref.shape[0], 2 * BLK), 0)).astype(F32)
    onehot = jnp.transpose(onehot).astype(BF)
    width = obs_ref.shape[1]
    part = 256

    def embed(n, _):
        cols = pl.ds(pl.multiple_of(n * part, part), part)
        added = jnp.dot(onehot, table_ref[:, cols], preferred_element_type=F32)
        tok[:, cols] = (obs_ref[:, cols].astype(F32) + added).astype(BF)
        return 0

    lax.fori_loop(0, width // part, embed, 0)

    def project(rows, w, out):
        def one(n, _):
            cols = pl.ds(pl.multiple_of(n * part, part), part)
            got = jnp.dot(rows, w[:, cols], preferred_element_type=F32).astype(BF)
            turned = jnp.transpose(got)
            out[0, cols, :] = turned[:, :BLK]
            out[1, cols, :] = turned[:, BLK:]
            return 0

        lax.fori_loop(0, width // part, one, 0)

    def there(step):
        return lax.rem(my_y + step // SIDE, SIDE), lax.rem(my_x + lax.rem(step, SIDE), SIDE)

    def back(step):
        return lax.rem(my_y + SIDE - step // SIDE, SIDE), lax.rem(my_x + SIDE - lax.rem(step, SIDE), SIDE)

    def head_rows(y, x):
        return pl.ds(pl.multiple_of((y * SIDE + x) * HD, HD), HD)

    def send(stage, buf, sends, recvs, step):
        y, x = there(step)
        return pltpu.make_async_remote_copy(
            src_ref=stage.at[:, head_rows(y, x), :],
            dst_ref=buf.at[pl.ds(me * 2, 2)],
            send_sem=sends.at[step], recv_sem=recvs.at[step],
            device_id={"agent": agent_at(y, x, core)}, device_id_type=MESH,
        )

    def arrival(stage, buf, sends, recvs, step):
        y, x = back(step)
        return pltpu.make_async_remote_copy(
            src_ref=stage.at[:, head_rows(y, x), :],
            dst_ref=buf.at[pl.ds(agent_at(y, x, core) * 2, 2)],
            send_sem=sends.at[step], recv_sem=recvs.at[step],
            device_id={"agent": agent_at(y, x, core)}, device_id_type=MESH,
        )

    def own_forward(stage, buf, sends, recvs):
        return pltpu.make_async_remote_copy(
            src_ref=stage.at[:, head_rows(my_y, my_x), :],
            dst_ref=buf.at[pl.ds(me * 2, 2)],
            send_sem=sends.at[0], recv_sem=recvs.at[0],
            device_id={"agent": sibling}, device_id_type=MESH,
        )

    def forward(buf, sends, recvs, step):
        y, x = back(step)
        slot = pl.ds(agent_at(y, x, core) * 2, 2)
        return pltpu.make_async_remote_copy(
            src_ref=buf.at[slot], dst_ref=buf.at[slot],
            send_sem=sends.at[step], recv_sem=recvs.at[step],
            device_id={"agent": sibling}, device_id_type=MESH,
        )

    def forwarded(buf, sends, recvs, step):
        y, x = back(step)
        slot = pl.ds(agent_at(y, x, 1 - core) * 2, 2)
        return pltpu.make_async_remote_copy(
            src_ref=buf.at[slot], dst_ref=buf.at[slot],
            send_sem=sends.at[step], recv_sem=recvs.at[step],
            device_id={"agent": sibling}, device_id_type=MESH,
        )

    def local(stage, buf, n):
        return pltpu.make_async_copy(
            stage.at[:, head_rows(my_y, my_x), :], buf.at[pl.ds(me * 2, 2)], local_sem.at[n]
        )

    def send_all(stage, buf, sends, recvs, fsends, frecvs, n):
        local(stage, buf, n).start()
        own_forward(stage, buf, fsends, frecvs).start()

        def one(step, _):
            send(stage, buf, sends, recvs, step).start()
            return 0

        lax.fori_loop(1, chips, one, 0)

    def q_send(step, flip):
        y, x = there(step)
        target = lax.rem(core + flip, 2)
        return pltpu.make_async_remote_copy(
            src_ref=qst.at[target, head_rows(y, x), :],
            dst_ref=qbuf.at[me],
            send_sem=qs_send.at[flip * chips + step], recv_sem=qs_recv.at[flip * chips + step],
            device_id={"agent": agent_at(y, x, target)}, device_id_type=MESH,
        )

    def q_arrival(step, flip):
        y, x = back(step)
        source = agent_at(y, x, lax.rem(core + flip, 2))
        return pltpu.make_async_remote_copy(
            src_ref=qst.at[core, head_rows(y, x), :],
            dst_ref=qbuf.at[source],
            send_sem=qs_send.at[flip * chips + step], recv_sem=qs_recv.at[flip * chips + step],
            device_id={"agent": source}, device_id_type=MESH,
        )

    loads[0].wait()
    project(tok[...], wk, kst)
    pl.semaphore_wait(barrier, 2 * chips - 1)
    send_all(kst, kbuf, ks_send, ks_recv, kf_send, kf_recv, 0)
    loads[1].wait()
    project(tok[...], wv, vst)
    send_all(vst, vbuf, vs_send, vs_recv, vf_send, vf_recv, 1)
    rows = jnp.concatenate(
        [obs_ref[0:HALF], obs_ref[BLK : BLK + HALF], obs_ref[HALF:BLK], obs_ref[BLK + HALF :]], axis=0
    )
    loads[2].wait()
    project(rows, wq, qst)
    q_local = pltpu.make_async_copy(qst.at[core, head_rows(my_y, my_x), :], qbuf.at[me], local_sem.at[2])
    q_local.start()
    q_send(0, 1).start()

    def q_one(step, _):
        q_send(step, 0).start()
        q_send(step, 1).start()
        return 0

    lax.fori_loop(1, chips, q_one, 0)

    def pass_on(stage, buf, sends, recvs, fsends, frecvs):
        def one(step, _):
            arrival(stage, buf, sends, recvs, step).wait_recv()
            forward(buf, fsends, frecvs, step).start()
            return 0

        lax.fori_loop(1, chips, one, 0)

    pass_on(kst, kbuf, ks_send, ks_recv, kf_send, kf_recv)
    pass_on(vst, vbuf, vs_send, vs_recv, vf_send, vf_recv)

    local(kst, kbuf, 0).wait()
    local(vst, vbuf, 1).wait()
    q_local.wait()
    own_forward(kst, kbuf, kf_send, kf_recv).wait_send()
    own_forward(vst, vbuf, vf_send, vf_recv).wait_send()
    forwarded(kbuf, kf_send, kf_recv, 0).wait_recv()
    forwarded(vbuf, vf_send, vf_recv, 0).wait_recv()
    q_send(0, 1).wait_send()
    q_arrival(0, 1).wait_recv()

    def finish(step, _):
        send(kst, kbuf, ks_send, ks_recv, step).wait_send()
        send(vst, vbuf, vs_send, vs_recv, step).wait_send()
        forward(kbuf, kf_send, kf_recv, step).wait_send()
        forward(vbuf, vf_send, vf_recv, step).wait_send()
        forwarded(kbuf, kf_send, kf_recv, step).wait_recv()
        forwarded(vbuf, vf_send, vf_recv, step).wait_recv()
        for flip in range(2):
            q_send(step, flip).wait_send()
            q_arrival(step, flip).wait_recv()
        return 0

    lax.fori_loop(1, chips, finish, 0)


def project(obs, actions, table, w_query, w_key, w_value):
    rows, width = obs.shape
    devices = 2 * SIDE * SIDE
    chips = SIDE * SIDE
    vm = pl.BlockSpec(memory_space=pltpu.VMEM)
    hbm = pl.BlockSpec(memory_space=pl.ANY)
    dma = pltpu.SemaphoreType.DMA
    return pl.pallas_call(
        project_kernel,
        out_shape=(
            jax.ShapeDtypeStruct((devices, HD, BLK), BF),
            jax.ShapeDtypeStruct((2 * devices, HD, BLK), BF),
            jax.ShapeDtypeStruct((2 * devices, HD, BLK), BF),
        ),
        in_specs=[vm, vm, vm] + [pl.BlockSpec(memory_space=pltpu.HBM)] * 3,
        out_specs=(hbm, hbm, hbm),
        scratch_shapes=[pltpu.VMEM((width, width), BF)] * 3
        + [pltpu.VMEM((rows, width), BF)]
        + [pltpu.VMEM((2, width, BLK), BF)] * 3
        + [dma((3,))]
        + [dma((chips,))] * 4
        + [dma((2 * chips,))] * 2
        + [dma((chips,))] * 4
        + [dma((3,))],
        compiler_params=pltpu.CompilerParams(
            collective_id=0, has_side_effects=True, vmem_limit_bytes=60 * 2**20
        ),
        name="project_and_send",
    )(obs, actions, table, w_query, w_key, w_value)


def attention_kernel(
    groups, steps,
    rank_ref, tile_ref, chunk_ref, rank_row, visible_ref, q_ref, k_ref, v_ref,
    o_ref,
    order, ks, vs, qa, acc, osort, sa, sb, mask,
):
    core = lax.rem(lax.axis_index("agent"), 2)
    blocks = k_ref.shape[0]
    per_tile = 4 * groups
    chunk_blocks = per_tile
    keys = chunk_blocks * BLK

    def place(b, _):
        order[rank_ref[b]] = b
        return 0

    lax.fori_loop(0, blocks, place, 0, unroll=4)

    lane = lax.broadcasted_iota(jnp.int32, (BLK, HD), 1)
    row = lax.broadcasted_iota(jnp.int32, (VROWS - HD, BLK), 0)
    ones = jnp.where(row == 0, 1.0, 0.0).astype(BF)

    def prepare(r, _):
        b = order[r]
        at = pl.multiple_of(r * BLK, BLK)
        hot = jnp.where(lane == r, 1.0, 0.0).astype(BF)
        ks[pl.ds(at, BLK), :] = jnp.concatenate([jnp.transpose(k_ref[b]), hot], axis=1)
        vs[r] = jnp.concatenate([v_ref[b], ones], axis=0)
        return 0

    lax.fori_loop(0, blocks, prepare, 0, unroll=4)

    ids_r = lax.broadcasted_iota(jnp.int32, (blocks, blocks), 0)
    ids_c = lax.broadcasted_iota(jnp.int32, (blocks, blocks), 1)
    to_rank = (ids_r == rank_row[...]).astype(BF)
    vis = visible_ref[...].astype(F32).astype(BF)
    by_query = jnp.dot(to_rank, vis, preferred_element_type=F32).astype(BF)
    ranked = lax.dot_general(
        by_query, to_rank, (((1,), (1,)), ((), ())), preferred_element_type=F32
    )
    sees = ((ids_r > ids_c) & (ranked > 0.5)) | (ids_r == ids_c)
    sees = jnp.transpose(jnp.where(sees, 1.0, 0.0)).astype(BF)

    qlane = lax.broadcasted_iota(jnp.int32, (HD, BLK), 1)
    spread_r = lax.broadcasted_iota(jnp.int32, (blocks, QN), 0)
    spread_c = lax.broadcasted_iota(jnp.int32, (blocks, QN), 1)

    def half(r, want):
        b = order[r]
        x = q_ref[b // 2].astype(F32)
        return jnp.where(jnp.full(x.shape, lax.rem(b, 2), jnp.int32) == want, x, pltpu.roll(x, HALF, 1))

    def prepare_queries(t, _):
        pieces = []
        for p in range(2):
            pieces.append(jnp.where(qlane < HALF, half(4 * t + 2 * p, 0), half(4 * t + 2 * p + 1, 1)))
        turned = (jnp.concatenate(pieces, axis=1) * HD**-0.5).astype(BF)
        spread = (spread_r == 4 * t + spread_c // HALF).astype(BF)
        open_ = jnp.dot(sees, spread, preferred_element_type=F32)
        bias = jnp.where(open_ > 0.5, 0.0, NEG).astype(BF)
        qa[t] = jnp.concatenate([turned, bias], axis=0)
        return 0

    lax.fori_loop(0, blocks // 4, prepare_queries, 0, unroll=2)

    mrow = lax.broadcasted_iota(jnp.int32, (2 * BLK, BLK), 0)
    mcol = lax.broadcasted_iota(jnp.int32, (2 * BLK, BLK), 1)
    late = (mrow // BLK == mcol // HALF) & (lax.rem(mrow, BLK) > lax.rem(mcol, HALF) + core * HALF)
    mask[0] = jnp.zeros((2 * BLK, BLK), F32)
    mask[1] = jnp.where(late, NEG, 0.0)
    acc[...] = jnp.zeros_like(acc)

    def score(i, buf):
        t, c = tile_ref[i], chunk_ref[i]
        diagonal = jnp.where(t == c, 1, 0)
        base = pl.multiple_of(c * keys, keys)
        peaks = []
        for g in range(groups):
            full = jnp.dot(ks[pl.ds(base, keys), :], qa[t * groups + g], preferred_element_type=F32)
            peak = None
            for blk in range(0, chunk_blocks, 2):
                rows = full[blk * BLK : (blk + 2) * BLK]
                p = blk // 2 - 2 * g
                if 0 <= p < 2:
                    cols = [rows[:, :BLK], rows[:, BLK:]]
                    cols[p] = cols[p] + mask[diagonal]
                    rows = jnp.concatenate(cols, axis=1)
                buf[g, blk * BLK : (blk + 2) * BLK] = rows
                top = jnp.max(rows.reshape(2 * BLK // 8, 8, QN), axis=0)
                peak = top if peak is None else jnp.maximum(peak, top)
            peaks.append(jnp.max(peak, axis=0, keepdims=True))
        return tuple(peaks)

    def absorb(i, buf, peaks, running):
        t, c = tile_ref[i], chunk_ref[i]
        new = []
        for g in range(groups):
            old = jnp.where(jnp.full((1, QN), c, jnp.int32) == 0, NEG, running[g])
            top = jnp.maximum(old, peaks[g])
            shrink = jnp.exp2((old - top) * LOG2E)
            expo = jnp.exp2((buf[g] - top) * LOG2E).astype(BF)
            vals = jnp.concatenate([vs[c * chunk_blocks + j] for j in range(chunk_blocks)], axis=1)
            acc[g] = acc[g] * shrink + jnp.dot(vals, expo, preferred_element_type=F32)
            new.append(top)

        @pl.when(c == t)
        def _():
            for g in range(groups):
                a = acc[g]
                out = a[:HD] / a[HD : HD + 1]
                for j in range(4):
                    osort[t * per_tile + g * 4 + j] = out[:, j * HALF : (j + 1) * HALF]

        return tuple(new)

    def two(h, carry):
        peaks, running = carry
        later = score(2 * h + 1, sb)
        running = absorb(2 * h, sa, peaks, running)
        peaks = score(2 * h + 2, sa)
        running = absorb(2 * h + 1, sb, later, running)
        return peaks, running

    running = tuple(jnp.full((1, QN), NEG, F32) for _ in range(groups))
    lax.fori_loop(0, steps // 2, two, (score(0, sa), running))

    def unsort(a, _):
        pair = [osort[rank_ref[2 * a]], osort[rank_ref[2 * a + 1]]]
        o_ref[a] = jnp.concatenate(pair, axis=1).astype(BF)
        return 0

    lax.fori_loop(0, blocks // 2, unsort, 0, unroll=2)


def attention(rank, visible, q, k, v, groups=2):
    blocks = k.shape[0]
    tiles = blocks // (4 * groups)
    plan = [(t, c) for t in range(tiles) for c in range(t + 1)]
    steps = len(plan)
    assert steps % 2 == 0
    plan.append((0, 0))
    tile_of = jnp.asarray(np.array([t for t, _ in plan], np.int32))
    chunk_of = jnp.asarray(np.array([c for _, c in plan], np.int32))
    keys = 4 * groups * BLK
    sm = pl.BlockSpec(memory_space=pltpu.SMEM)
    vm = pl.BlockSpec(memory_space=pltpu.VMEM)
    return pl.pallas_call(
        functools.partial(attention_kernel, groups, steps),
        out_shape=jax.ShapeDtypeStruct((blocks // 2, HD, BLK), BF),
        in_specs=[sm] * 3 + [vm] * 5,
        out_specs=vm,
        scratch_shapes=[
            pltpu.SMEM((blocks,), jnp.int32),
            pltpu.VMEM((blocks * BLK, HD + blocks), BF),
            pltpu.VMEM((blocks, VROWS, BLK), BF),
            pltpu.VMEM((blocks // 4, HD + blocks, QN), BF),
            pltpu.VMEM((groups, VROWS, QN), F32),
            pltpu.VMEM((blocks, HD, HALF), F32),
            pltpu.VMEM((groups, keys, QN), F32),
            pltpu.VMEM((groups, keys, QN), F32),
            pltpu.VMEM((2, 2 * BLK, BLK), F32),
        ],
        compiler_params=pltpu.CompilerParams(vmem_limit_bytes=48 * 2**20),
        name="attention",
    )(rank, tile_of, chunk_of, rank[None, :], visible, q, k, v)


def head_kernel(
    group_ref, o_hbm, obs_ref, gain_ref, whead_ref, ret_ref, wo, wm, wg,
    val_ref, adv_ref,
    att, resid, hid, hbuf, mix, part,
    a_send, a_recv, z_send, z_recv, local_sem,
):
    me = lax.axis_index("agent")
    env = lax.axis_index("env")
    envs = hbuf.shape[0]
    core = lax.rem(me, 2)
    chip = me // 2
    my_y, my_x = chip // SIDE, lax.rem(chip, SIDE)
    chips = SIDE * SIDE
    barrier = greet_plane(me)

    def tell(step, _):
        other = lax.rem(env + step, envs)
        pl.semaphore_signal(barrier, inc=1, device_id={"env": other}, device_id_type=MESH)
        return 0

    lax.fori_loop(1, envs, tell, 0)
    pl.semaphore_wait(barrier, 2 * chips - 1 + envs - 1)

    def send(step, flip):
        y = lax.rem(my_y + step // SIDE, SIDE)
        x = lax.rem(my_x + lax.rem(step, SIDE), SIDE)
        target = agent_at(y, x, lax.rem(core + flip, 2))
        return pltpu.make_async_remote_copy(
            src_ref=o_hbm.at[target], dst_ref=att.at[core, chip],
            send_sem=a_send.at[flip * chips + step], recv_sem=a_recv.at[flip * chips + step],
            device_id={"agent": target}, device_id_type=MESH,
        )

    def arrival(step, flip):
        y = lax.rem(my_y + SIDE - step // SIDE, SIDE)
        x = lax.rem(my_x + SIDE - lax.rem(step, SIDE), SIDE)
        other = lax.rem(core + flip, 2)
        return pltpu.make_async_remote_copy(
            src_ref=o_hbm.at[me], dst_ref=att.at[other, y * SIDE + x],
            send_sem=a_send.at[flip * chips + step], recv_sem=a_recv.at[flip * chips + step],
            device_id={"agent": agent_at(y, x, other)}, device_id_type=MESH,
        )

    own = pltpu.make_async_copy(o_hbm.at[me], att.at[core, chip], local_sem.at[0])
    own.start()
    send(0, 1).start()

    def start(step, _):
        send(step, 0).start()
        send(step, 1).start()
        return 0

    lax.fori_loop(1, chips, start, 0)
    own.wait()
    arrival(0, 1).wait_recv()

    def land(step, _):
        arrival(step, 0).wait_recv()
        arrival(step, 1).wait_recv()
        return 0

    lax.fori_loop(1, chips, land, 0)

    width = obs_ref.shape[1]
    wide = 256
    for half in range(2):
        rows = jnp.transpose(att[half].reshape(width, BLK))
        seen = jnp.concatenate(
            [obs_ref[half * HALF : (half + 1) * HALF], obs_ref[BLK + half * HALF : BLK + (half + 1) * HALF]], axis=0
        ).astype(F32)
        for n in range(width // wide):
            cols = slice(n * wide, (n + 1) * wide)
            resid[half * BLK : (half + 1) * BLK, cols] = seen[:, cols] + jnp.dot(
                rows, wo[:, cols], preferred_element_type=F32
            )
    whole = resid[...]
    factor = lax.rsqrt(jnp.mean(whole * whole, axis=1, keepdims=True) + 1e-05)
    hid[...] = (whole * factor * gain_ref[...]).astype(BF)

    per_env = 2 * BLK // envs

    def piece(e):
        quarter = lax.rem(e, 4)
        return pl.ds(pl.multiple_of(quarter // 2 * BLK + e // 4 * HALF + lax.rem(quarter, 2) * per_env, per_env), per_env)

    def z_copy(step):
        other = lax.rem(env + step, envs)
        return pltpu.make_async_remote_copy(
            src_ref=hid.at[piece(other)], dst_ref=hbuf.at[env],
            send_sem=z_send.at[step], recv_sem=z_recv.at[step],
            device_id={"env": other}, device_id_type=MESH,
        )

    def z_arrival(step):
        other = lax.rem(env + envs - step, envs)
        return pltpu.make_async_remote_copy(
            src_ref=hid.at[piece(env)], dst_ref=hbuf.at[other],
            send_sem=z_send.at[step], recv_sem=z_recv.at[step],
            device_id={"env": other}, device_id_type=MESH,
        )

    mine = pltpu.make_async_copy(hid.at[piece(env)], hbuf.at[env], local_sem.at[1])
    mine.start()

    def z_start(step, _):
        z_copy(step).start()
        return 0

    lax.fori_loop(1, envs, z_start, 0)
    mine.wait()

    def z_land(step, _):
        z_arrival(step).wait_recv()
        return 0

    lax.fori_loop(1, envs, z_land, 0)

    moved = hbuf[...].reshape(envs * per_env, width)
    hidden_units = whead_ref.shape[1]
    for n in range(hidden_units // wide):
        cols = slice(n * wide, (n + 1) * wide)
        mix[:, :, cols] = jnp.dot(moved, wm[:, cols], preferred_element_type=F32).reshape(envs, per_env, wide)
        part[:, :, cols] = jnp.dot(moved, wg[:, cols], preferred_element_type=F32).reshape(envs, per_env, wide)
    partners = []
    values = []
    for e in range(envs):
        partner = jnp.int32(0)
        for f in range(envs):
            if f != e:
                partner = jnp.where(group_ref[f] == group_ref[e], f, partner)
        partners.append(partner)
        x = mix[e] + 0.5 * (part[e] + part[partner])
        activ = 0.5 * x * (1.0 + lax.erf(x * np.float32(np.sqrt(0.5))))
        values.append(jnp.sum(activ * whead_ref[...], axis=1, keepdims=True).T)
    for e in range(envs):
        val_ref[e : e + 1, :] = values[e]
    excess = ret_ref[...] - val_ref[...]
    rows = lax.broadcasted_iota(jnp.int32, (envs, per_env), 0)
    for e in range(envs):
        mine_ = excess[e : e + 1]
        other = jnp.sum(jnp.where(rows == jnp.full(rows.shape, partners[e], jnp.int32), excess, 0.0), axis=0, keepdims=True)
        adv_ref[e : e + 1, :] = mine_ - 0.5 * (mine_ + other)

    send(0, 1).wait_send()

    def finish(step, _):
        send(step, 0).wait_send()
        send(step, 1).wait_send()
        return 0

    lax.fori_loop(1, chips, finish, 0)

    def z_finish(step, _):
        z_copy(step).wait_send()
        return 0

    lax.fori_loop(1, envs, z_finish, 0)


def head(group_of_env, o, obs, gain, w_head, returns, w_out, w_mix, w_group):
    rows, width = obs.shape
    envs, per_env = returns.shape
    units = w_head.shape[0]
    chips = SIDE * SIDE
    sm = pl.BlockSpec(memory_space=pltpu.SMEM)
    vm = pl.BlockSpec(memory_space=pltpu.VMEM)
    hbm = pl.BlockSpec(memory_space=pl.ANY)
    dma = pltpu.SemaphoreType.DMA
    out = jax.ShapeDtypeStruct((envs, per_env), F32)
    return pl.pallas_call(
        head_kernel,
        out_shape=(out, out),
        in_specs=[sm, hbm] + [vm] * 7,
        out_specs=(vm, vm),
        scratch_shapes=[
            pltpu.VMEM((2, chips, HD, BLK), BF),
            pltpu.VMEM((rows, width), F32),
            pltpu.VMEM((rows, width), BF),
            pltpu.VMEM((envs, per_env, width), BF),
            pltpu.VMEM((envs, per_env, units), F32),
            pltpu.VMEM((envs, per_env, units), F32),
            dma((2 * chips,)),
            dma((2 * chips,)),
            dma((envs,)),
            dma((envs,)),
            dma((2,)),
        ],
        compiler_params=pltpu.CompilerParams(
            collective_id=1, has_side_effects=True, vmem_limit_bytes=40 * 2**20
        ),
        name="rows_and_value",
    )(group_of_env, o, obs, gain[None, :], w_head[None, :], returns, w_out, w_mix, w_group)


def on_device(
    obs_rep, actions, action_table, decode_rank, visible, w_query, w_key, w_value, w_out,
    norm_gain, w_mix, w_group, w_head, returns, group_of_env,
):
    obs = obs_rep[0]
    q, k, v = project(obs, actions, action_table, w_query, w_key, w_value)
    o = attention(decode_rank, visible, q, k, v)
    return head(group_of_env, o, obs, norm_gain, w_head, returns, w_out, w_mix, w_group)


def solution(mesh):
    spec = P(None, ("agent", "env"))
    in_specs = (P("env", "agent", None), P("env", "agent")) + (P(),) * 11 + (spec, P())
    return jax.shard_map(
        on_device, mesh=mesh, in_specs=in_specs, out_specs=(spec, spec), check_vma=False
    )
```

profile of v0, /device:TPU:64, one launch (start us, length us, event | category | flops | bytes accessed | tf_op | source)
XLA Modules:
  0.0 99.3 jit_solution(3208408803527484077)
XLA Ops:
  0.6 0.0 copy-start.7
  0.6 0.0 copy-start.11
  0.7 0.0 copy-start.13
  0.7 0.0 copy-start.14
  0.7 0.0 copy-start.2
  0.7 0.0 copy-start.3
  0.7 0.0 copy-start.8
  0.7 0.0 copy-start.9
  0.7 0.0 copy-start.10
  0.7 0.0 copy-start.12
  0.7 28.8 %project_and_send.1 = (bf16[32,64,128]{2,1,0:T(8,128)(2,1)}, bf16[64,64,128]{2,1,0:T(8,128)(2,1)}, bf16[64,64,128]{2,1,0:T(8,128)(2,1)}) custom-call(bf16[256,1024]{1,0:T(8,128)(2,1)} %bitcast.4, s32[1,256]{1,0:T(1,128)} %act_ref.1, bf16[32,1024]{1,0:T(8,128)(2,1)} %table_ref.1, bf16[1024,1024]{1,0:T(8,128)(2,1)} %wq_hbm.1, bf16[1024,1024]{1,0:T(8,128)(2,1)} %wk_hbm.1, ...), custom_call_target="tpu_custom_call" | custom-call | tf_op jit(solution)/shard_map/project_and_send/pallas_call | solution.py:239
  29.6 0.0 copy-start
  29.6 0.0 copy-start.1
  29.6 0.0 copy-done.7
  29.6 0.0 copy-done.11
  29.6 0.0 copy-done.13
  29.6 0.0 copy-done.14
  29.7 0.0 copy-start.4
  29.7 1.4 %copy-done.4 = bf16[64,64,128]{2,1,0:T(8,128)(2,1)S(1)} copy-done((bf16[64,64,128]{2,1,0:T(8,128)(2,1)S(1)}, bf16[64,64,128]{2,1,0:T(8,128)(2,1)}, u32[]{:S(2)}) %copy-start.4) | copy-done | bytes 1048600
  31.0 1.2 %copy-done.5 = bf16[64,64,128]{2,1,0:T(8,128)(2,1)S(1)} copy-done((bf16[64,64,128]{2,1,0:T(8,128)(2,1)S(1)}, bf16[64,64,128]{2,1,0:T(8,128)(2,1)}, u32[]{:S(2)}) %copy-start.5) | copy-done | bytes 1048600
  32.3 1.0 %copy-done.6 = bf16[32,64,128]{2,1,0:T(8,128)(2,1)S(1)} copy-done((bf16[32,64,128]{2,1,0:T(8,128)(2,1)S(1)}, bf16[32,64,128]{2,1,0:T(8,128)(2,1)}, u32[]{:S(2)}) %copy-start.6) | copy-done | bytes 524312
  33.3 30.5 %attention.1.o_hbm = bf16[32,64,128]{2,1,0:T(8,128)(2,1)S(1)} custom-call(s32[64]{0:T(128)S(1)} %copy-done.11, s32[37]{0:T(128)S(1)} %copy-done.14, s32[37]{0:T(128)S(1)} %copy-done.13, s32[1,64]{1,0:T(1,128)S(1)} %bitcast.8, s32[64,64]{1,0:T(8,128)S(1)} %copy-done.7, bf16[32,64,128]{2,1,0:T(8,128)(2,1)S(1)} %copy-done.6, ...), custom_call_target="tpu_custom_call" | custom-call | tf_op jit(solution)/shard_map/attention/pallas_call | solution.py:409
  63.8 0.0 copy-done.2
  63.8 0.0 copy-done.3
  63.8 0.0 copy-done.8
  63.8 0.0 copy-done.9
  63.8 0.0 copy-done.10
  63.9 0.0 copy-done.12
  63.9 0.0 copy-done
  63.9 34.2 %rows_and_value.1 = (f32[8,32]{1,0:T(8,128)S(1)}, f32[8,32]{1,0:T(8,128)S(1)}) custom-call(s32[8]{0:T(128)S(1)} %copy-done.12, bf16[32,64,128]{2,1,0:T(8,128)(2,1)S(1)} %attention.1.o_hbm, bf16[256,1024]{1,0:T(8,128)(2,1)S(1)} %bitcast.5, f32[1,1024]{1,0:T(1,128)S(1)} %bitcast.6, f32[1,512]{1,0:T(1,128)S(1)} %bitcast.7, f32[8,32]{1,0:T(8,128)S(1)} %copy-done.9, ...), custom_call_target="tpu_custom_call" | custom-call | tf_op jit(solution)/shard_map/rows_and_value/pallas_call | solution.py:599
  98.1 0.6 copy.21
  98.7 0.6 copy.22
  (3 shorter events, 0.0 us)
Async XLA Ops:
  0.6 29.0 %copy-start.7 = (s32[64,64]{1,0:T(8,128)S(1)}, s32[64,64]{1,0:T(8,128)}, u32[]{:S(2)}) copy-start(s32[64,64]{1,0:T(8,128)} %visible_ref.1) | copy-start | bytes 49156
  0.6 29.0 %copy-start.11 = (s32[64]{0:T(128)S(1)}, s32[64]{0:T(128)}, u32[]{:S(2)}) copy-start(s32[64]{0:T(128)} %rank_ref.1) | copy-start | bytes 772
  0.7 29.0 %copy-start.13 = (s32[37]{0:T(128)S(1)}, s32[37]{0:T(128)}, u32[]{:S(2)}) copy-start(s32[37]{0:T(128)} %constant.5.clone.chunk_ref) | copy-start | bytes 448
  0.7 29.0 %copy-start.14 = (s32[37]{0:T(128)S(1)}, s32[37]{0:T(128)}, u32[]{:S(2)}) copy-start(s32[37]{0:T(128)} %constant.4.clone.tile_ref) | copy-start | bytes 448
  0.7 63.1 %copy-start.2 = (bf16[1024,512]{1,0:T(8,128)(2,1)S(1)}, bf16[1024,512]{1,0:T(8,128)(2,1)}, u32[]{:S(2)}) copy-start(bf16[1024,512]{1,0:T(8,128)(2,1)} %wm.1) | copy-start | bytes 3145732
  0.7 63.1 %copy-start.3 = (bf16[1024,512]{1,0:T(8,128)(2,1)S(1)}, bf16[1024,512]{1,0:T(8,128)(2,1)}, u32[]{:S(2)}) copy-start(bf16[1024,512]{1,0:T(8,128)(2,1)} %wg.1) | copy-start | bytes 3145732
  0.7 63.1 %copy-start.8 = (f32[1024]{0:T(1024)S(1)}, f32[1024]{0:T(1024)}, u32[]{:S(2)}) copy-start(f32[1024]{0:T(1024)} %param.26) | copy-start | bytes 12292
  0.7 63.1 %copy-start.9 = (f32[8,32]{1,0:T(8,128)S(1)}, f32[8,32]{1,0:T(8,128)}, u32[]{:S(2)}) copy-start(f32[8,32]{1,0:T(8,128)} %ret_ref.1) | copy-start | bytes 3076
  0.7 63.1 %copy-start.10 = (f32[512]{0:T(512)S(1)}, f32[512]{0:T(512)}, u32[]{:S(2)}) copy-start(f32[512]{0:T(512)} %param.29) | copy-start | bytes 6148
  0.7 63.1 %copy-start.12 = (s32[8]{0:T(128)S(1)}, s32[8]{0:T(128)}, u32[]{:S(2)}) copy-start(s32[8]{0:T(128)} %group_ref.1) | copy-start | bytes 100
  29.6 34.3 %copy-start = (bf16[1,256,1024]{2,1,0:T(8,128)(2,1)S(1)}, bf16[1,256,1024]{2,1,0:T(8,128)(2,1)}, u32[]{:S(2)}) copy-start(bf16[1,256,1024]{2,1,0:T(8,128)(2,1)} %param.17) | copy-start | bytes 1572868
  29.6 34.3 %copy-start.1 = (bf16[1024,1024]{1,0:T(8,128)(2,1)S(1)}, bf16[1024,1024]{1,0:T(8,128)(2,1)}, u32[]{:S(2)}) copy-start(bf16[1024,1024]{1,0:T(8,128)(2,1)} %wo.1) | copy-start | bytes 6291460
  29.7 1.4 %copy-start.4 = (bf16[64,64,128]{2,1,0:T(8,128)(2,1)S(1)}, bf16[64,64,128]{2,1,0:T(8,128)(2,1)}, u32[]{:S(2)}) copy-start(bf16[64,64,128]{2,1,0:T(8,128)(2,1)} %get-tuple-element.6.k_ref) | copy-start | bytes 3145732
  31.0 1.2 %copy-start.5 = (bf16[64,64,128]{2,1,0:T(8,128)(2,1)S(1)}, bf16[64,64,128]{2,1,0:T(8,128)(2,1)}, u32[]{:S(2)}) copy-start(bf16[64,64,128]{2,1,0:T(8,128)(2,1)} %get-tuple-element.7.v_ref) | copy-start | bytes 3145732
  32.3 1.0 %copy-start.6 = (bf16[32,64,128]{2,1,0:T(8,128)(2,1)S(1)}, bf16[32,64,128]{2,1,0:T(8,128)(2,1)}, u32[]{:S(2)}) copy-start(bf16[32,64,128]{2,1,0:T(8,128)(2,1)} %get-tuple-element.5.q_ref) | copy-start | bytes 1572868
where the time goes:
time: 99.9 us; the launch traced here: 99.3 us
  Pallas kernels  93.5 us (94%)
  local copies, waits for them, and re-layouts  4.88 us (5%)
    pallas_call x1, Pallas kernels, head(): pl.pallas_call(head_kernel, out_shape=(out, out), in_specs=[sm, hbm] + [v...  34.2 us
    pallas_call x1, Pallas kernels, attention(): pl.pallas_call(functools.partial(attention_kernel, groups, steps), out_sh...  30.5 us
    pallas_call x1, Pallas kernels, project(): pl.pallas_call(project_kernel, out_shape=(jax.ShapeDtypeStruct((devices,...  28.8 us
    unnamed x32, local copies, waits for them, and re-layouts  4.88 us

commit v1 on v0

v1 whole, which is shorter than its diff:
```python
import jax
import jax.numpy as jnp
import numpy as np
from jax import lax
from jax.experimental import pallas as pl
from jax.experimental.pallas import tpu as pltpu
from jax.sharding import PartitionSpec as P

H = 16
BLK = 128
HALF = BLK // 2
HD = 64
LOG2E = 1.4426950408889634
NEG = -1e30
VROWS = 80
QN = 256
SIDE = 4
MESH = pl.DeviceIdType.MESH
BF = jnp.bfloat16
F32 = jnp.float32


def agent_at(y, x, core):
    return (y * SIDE + x) * 2 + core


OFFSETS = (
    (0, 1), (0, 3), (1, 0), (3, 0), (0, 2), (2, 0), (1, 1), (3, 3),
    (1, 3), (3, 1), (1, 2), (3, 2), (2, 1), (2, 3), (2, 2),
)
RING = (1, 7, 2, 6, 3, 5, 4)


def pick(n, values):
    got = jnp.int32(values[0])
    for at, value in enumerate(values[1:], 1):
        got = jnp.where(n == at, value, got)
    return got


def chip_step(n):
    return pick(n, (0,) + tuple(y * SIDE + x for y, x in OFFSETS))


def decoder_kernel(
    rank_ref, order, group_ref, rank_row, visible_ref, obs_ref, act_ref, table_ref, gain_ref, whead_ref, ret_ref,
    wq_hbm, wk_hbm, wv_hbm, wo_hbm, wm_hbm, wg_hbm,
    val_ref, adv_ref,
    wq, wk, wv, wo, wm, wg, tok, kst, vst, qst, qbuf, kbuf, vbuf,
    ks, vs, qa, acc, osort, ost, sa, sb, mask,
    att, resid, hid, hbuf, mix, part,
    load_sem, ks_send, ks_recv, vs_send, vs_recv, qs_send, qs_recv, kf_send, kf_recv, vf_send, vf_recv,
    a_send, a_recv, z_send, z_recv, local_sem,
):
    groups = acc.shape[0]
    env = lax.axis_index("env")
    envs = hbuf.shape[0]
    me = lax.axis_index("agent")
    core = lax.rem(me, 2)
    chip = me // 2
    my_y, my_x = chip // SIDE, lax.rem(chip, SIDE)
    chips = SIDE * SIDE
    sibling = chip * 2 + 1 - core
    pairs = ((wk_hbm, wk), (wv_hbm, wv), (wq_hbm, wq), (wo_hbm, wo), (wm_hbm, wm), (wg_hbm, wg))
    loads = [pltpu.make_async_copy(src, dst, load_sem.at[n]) for n, (src, dst) in enumerate(pairs)]
    for load in loads[:3]:
        load.start()
    barrier = pltpu.get_barrier_semaphore()

    def tell(step, _):
        other = lax.rem(me + step, 2 * chips)
        pl.semaphore_signal(barrier, inc=1, device_id={"agent": other}, device_id_type=MESH)
        return 0

    def tell_env(step, _):
        other = lax.rem(env + step, envs)
        pl.semaphore_signal(barrier, inc=1, device_id={"env": other}, device_id_type=MESH)
        return 0

    lax.fori_loop(1, 2 * chips, tell, 0)
    lax.fori_loop(1, envs, tell_env, 0)

    blocks = rank_row.shape[1]
    ids_r = lax.broadcasted_iota(jnp.int32, (blocks, blocks), 0)
    ids_c = lax.broadcasted_iota(jnp.int32, (blocks, blocks), 1)
    to_rank = (ids_r == rank_row[...]).astype(F32)

    onehot = (act_ref[...] == lax.broadcasted_iota(jnp.int32, (table_ref.shape[0], 2 * BLK), 0)).astype(F32)
    onehot = jnp.transpose(onehot).astype(BF)
    width = obs_ref.shape[1]
    strip = 256

    def embed(n, _):
        cols = pl.ds(pl.multiple_of(n * strip, strip), strip)
        added = jnp.dot(onehot, table_ref[:, cols], preferred_element_type=F32)
        tok[:, cols] = (obs_ref[:, cols].astype(F32) + added).astype(BF)
        return 0

    lax.fori_loop(0, width // strip, embed, 0)

    def project(rows, w, out):
        def one(n, _):
            cols = pl.ds(pl.multiple_of(n * strip, strip), strip)
            got = jnp.dot(rows, w[:, cols], preferred_element_type=F32).astype(BF)
            turned = jnp.transpose(got)
            out[0, cols, :] = turned[:, :BLK]
            out[1, cols, :] = turned[:, BLK:]
            return 0

        lax.fori_loop(0, width // strip, one, 0)

    def there(step):
        return lax.rem(my_y + step // SIDE, SIDE), lax.rem(my_x + lax.rem(step, SIDE), SIDE)

    def back(step):
        return lax.rem(my_y + SIDE - step // SIDE, SIDE), lax.rem(my_x + SIDE - lax.rem(step, SIDE), SIDE)

    def head_rows(y, x):
        return pl.ds(pl.multiple_of((y * SIDE + x) * HD, HD), HD)

    def send(stage, buf, sends, recvs, step):
        y, x = there(step)
        return pltpu.make_async_remote_copy(
            src_ref=stage.at[:, head_rows(y, x), :],
            dst_ref=buf.at[pl.ds(me * 2, 2)],
            send_sem=sends.at[step], recv_sem=recvs.at[step],
            device_id={"agent": agent_at(y, x, core)}, device_id_type=MESH,
        )

    def arrival(stage, buf, sends, recvs, step):
        y, x = back(step)
        return pltpu.make_async_remote_copy(
            src_ref=stage.at[:, head_rows(y, x), :],
            dst_ref=buf.at[pl.ds(agent_at(y, x, core) * 2, 2)],
            send_sem=sends.at[step], recv_sem=recvs.at[step],
            device_id={"agent": agent_at(y, x, core)}, device_id_type=MESH,
        )

    def own_forward(stage, buf, sends, recvs):
        return pltpu.make_async_remote_copy(
            src_ref=stage.at[:, head_rows(my_y, my_x), :],
            dst_ref=buf.at[pl.ds(me * 2, 2)],
            send_sem=sends.at[0], recv_sem=recvs.at[0],
            device_id={"agent": sibling}, device_id_type=MESH,
        )

    def forward(buf, sends, recvs, step):
        y, x = back(step)
        slot = pl.ds(agent_at(y, x, core) * 2, 2)
        return pltpu.make_async_remote_copy(
            src_ref=buf.at[slot], dst_ref=buf.at[slot],
            send_sem=sends.at[step], recv_sem=recvs.at[step],
            device_id={"agent": sibling}, device_id_type=MESH,
        )

    def forwarded(buf, sends, recvs, step):
        y, x = back(step)
        slot = pl.ds(agent_at(y, x, 1 - core) * 2, 2)
        return pltpu.make_async_remote_copy(
            src_ref=buf.at[slot], dst_ref=buf.at[slot],
            send_sem=sends.at[step], recv_sem=recvs.at[step],
            device_id={"agent": sibling}, device_id_type=MESH,
        )

    def local(stage, buf, n):
        return pltpu.make_async_copy(
            stage.at[:, head_rows(my_y, my_x), :], buf.at[pl.ds(me * 2, 2)], local_sem.at[n]
        )

    def send_all(stage, buf, sends, recvs, fsends, frecvs, n):
        local(stage, buf, n).start()
        own_forward(stage, buf, fsends, frecvs).start()

        def one(n, _):
            send(stage, buf, sends, recvs, chip_step(n)).start()
            return 0

        lax.fori_loop(1, chips, one, 0)

    def q_send(step, flip):
        y, x = there(step)
        target = lax.rem(core + flip, 2)
        return pltpu.make_async_remote_copy(
            src_ref=qst.at[target, head_rows(y, x), :],
            dst_ref=qbuf.at[me],
            send_sem=qs_send.at[flip * chips + step], recv_sem=qs_recv.at[flip * chips + step],
            device_id={"agent": agent_at(y, x, target)}, device_id_type=MESH,
        )

    def q_arrival(step, flip):
        y, x = back(step)
        source = agent_at(y, x, lax.rem(core + flip, 2))
        return pltpu.make_async_remote_copy(
            src_ref=qst.at[core, head_rows(y, x), :],
            dst_ref=qbuf.at[source],
            send_sem=qs_send.at[flip * chips + step], recv_sem=qs_recv.at[flip * chips + step],
            device_id={"agent": source}, device_id_type=MESH,
        )

    loads[0].wait()
    project(tok[...], wk, kst)
    pl.semaphore_wait(barrier, 2 * chips - 1 + envs - 1)
    for load in loads[3:]:
        load.start()
    send_all(kst, kbuf, ks_send, ks_recv, kf_send, kf_recv, 0)
    loads[1].wait()
    project(tok[...], wv, vst)
    send_all(vst, vbuf, vs_send, vs_recv, vf_send, vf_recv, 1)
    rows = jnp.concatenate(
        [obs_ref[0:HALF], obs_ref[BLK : BLK + HALF], obs_ref[HALF:BLK], obs_ref[BLK + HALF :]], axis=0
    )
    loads[2].wait()
    project(rows, wq, qst)
    q_local = pltpu.make_async_copy(qst.at[core, head_rows(my_y, my_x), :], qbuf.at[me], local_sem.at[2])
    q_local.start()
    q_send(0, 1).start()

    def q_one(n, _):
        step = chip_step(n)
        q_send(step, 0).start()
        q_send(step, 1).start()
        return 0

    lax.fori_loop(1, chips, q_one, 0)

    def pass_on(stage, buf, sends, recvs, fsends, frecvs):
        def one(n, _):
            step = chip_step(n)
            arrival(stage, buf, sends, recvs, step).wait_recv()
            forward(buf, fsends, frecvs, step).start()
            return 0

        def two(step, _):
            forwarded(buf, fsends, frecvs, step).wait_recv()
            return 0

        lax.fori_loop(1, chips, one, 0)
        lax.fori_loop(0, chips, two, 0)

    lane = lax.broadcasted_iota(jnp.int32, (BLK, HD), 1)
    row = lax.broadcasted_iota(jnp.int32, (VROWS - HD, BLK), 0)
    ones = jnp.where(row == 0, 1.0, 0.0).astype(BF)

    def prepare_keys(r, _):
        at = pl.multiple_of(r * BLK, BLK)
        hot = jnp.where(lane == r, 1.0, 0.0).astype(BF)
        ks[pl.ds(at, BLK), :] = jnp.concatenate([jnp.transpose(kbuf[order[r]]), hot], axis=1)
        return 0

    def prepare_values(r, _):
        vs[r] = jnp.concatenate([vbuf[order[r]], ones], axis=0)
        return 0

    to_rank = to_rank.astype(BF)
    vis = visible_ref[...].astype(F32).astype(BF)
    by_query = jnp.dot(to_rank, vis, preferred_element_type=F32).astype(BF)
    ranked = lax.dot_general(
        by_query, to_rank, (((1,), (1,)), ((), ())), preferred_element_type=F32
    )
    sees = ((ids_r > ids_c) & (ranked > 0.5)) | (ids_r == ids_c)
    sees = jnp.transpose(jnp.where(sees, 1.0, 0.0)).astype(BF)

    mrow = lax.broadcasted_iota(jnp.int32, (2 * BLK, BLK), 0)
    mcol = lax.broadcasted_iota(jnp.int32, (2 * BLK, BLK), 1)
    late = (mrow // BLK == mcol // HALF) & (lax.rem(mrow, BLK) > lax.rem(mcol, HALF) + core * HALF)
    mask[0] = jnp.zeros((2 * BLK, BLK), F32)
    mask[1] = jnp.where(late, NEG, 0.0)
    acc[...] = jnp.zeros_like(acc)

    qlane = lax.broadcasted_iota(jnp.int32, (HD, BLK), 1)
    spread_r = lax.broadcasted_iota(jnp.int32, (blocks, QN), 0)
    spread_c = lax.broadcasted_iota(jnp.int32, (blocks, QN), 1)

    def half(r, want):
        b = order[r]
        x = qbuf[b // 2].astype(F32)
        return jnp.where(jnp.full(x.shape, lax.rem(b, 2), jnp.int32) == want, x, pltpu.roll(x, HALF, 1))

    def prepare_queries(t, _):
        pieces = []
        for p in range(2):
            pieces.append(jnp.where(qlane < HALF, half(4 * t + 2 * p, 0), half(4 * t + 2 * p + 1, 1)))
        turned = (jnp.concatenate(pieces, axis=1) * HD**-0.5).astype(BF)
        spread = (spread_r == 4 * t + spread_c // HALF).astype(BF)
        open_ = jnp.dot(sees, spread, preferred_element_type=F32)
        bias = jnp.where(open_ > 0.5, 0.0, NEG).astype(BF)
        qa[t] = jnp.concatenate([turned, bias], axis=0)
        return 0

    per_tile = 4 * groups
    chunk_blocks = per_tile
    keys = chunk_blocks * BLK
    tiles = blocks // per_tile

    def place_of(i):
        p, j = i // (tiles + 1), lax.rem(i, tiles + 1)
        first = j < p + 1
        return jnp.where(first, p, tiles - 1 - p), jnp.where(first, j, j - p - 1)

    pass_on(kst, kbuf, ks_send, ks_recv, kf_send, kf_recv)
    local(kst, kbuf, 0).wait()
    lax.fori_loop(0, blocks, prepare_keys, 0, unroll=4)
    pass_on(vst, vbuf, vs_send, vs_recv, vf_send, vf_recv)
    local(vst, vbuf, 1).wait()
    lax.fori_loop(0, blocks, prepare_values, 0, unroll=4)
    q_local.wait()
    q_arrival(0, 1).wait_recv()

    def q_land(step, _):
        q_arrival(step, 0).wait_recv()
        q_arrival(step, 1).wait_recv()
        return 0

    lax.fori_loop(1, chips, q_land, 0)
    lax.fori_loop(0, blocks // 4, prepare_queries, 0, unroll=2)

    def score(i, buf, which):
        t, c = place_of(i)
        diagonal = jnp.where(t == c, 1, 0)
        base = pl.multiple_of(c * keys, keys)
        peaks = []
        for g in which:
            full = jnp.dot(ks[pl.ds(base, keys), :], qa[t * groups + g], preferred_element_type=F32)
            peak = None
            for blk in range(0, chunk_blocks, 2):
                rows = full[blk * BLK : (blk + 2) * BLK]
                p = blk // 2 - 2 * g
                if 0 <= p < 2:
                    cols = [rows[:, :BLK], rows[:, BLK:]]
                    cols[p] = cols[p] + mask[diagonal]
                    rows = jnp.concatenate(cols, axis=1)
                buf[g, blk * BLK : (blk + 2) * BLK] = rows
                top = jnp.max(rows.reshape(2 * BLK // 8, 8, QN), axis=0)
                peak = top if peak is None else jnp.maximum(peak, top)
            peaks.append(jnp.max(peak, axis=0, keepdims=True))
        return tuple(peaks)

    def absorb(i, buf, peaks, running, which):
        t, c = place_of(i)
        new = []
        for g, peak, before in zip(which, peaks, running):
            old = jnp.where(jnp.full((1, QN), c, jnp.int32) == 0, NEG, before)
            top = jnp.maximum(old, peak)
            shrink = jnp.exp2((old - top) * LOG2E)
            expo = jnp.exp2((buf[g] - top) * LOG2E).astype(BF)
            vals = jnp.concatenate([vs[c * chunk_blocks + j] for j in range(chunk_blocks)], axis=1)
            acc[g] = acc[g] * shrink + jnp.dot(vals, expo, preferred_element_type=F32)
            new.append(top)

        return tuple(new)

    def finish_tile(i):
        t, c = place_of(i)

        @pl.when(c == t)
        def _():
            for g in range(groups):
                a = acc[g]
                out = a[:HD] / a[HD : HD + 1]
                for j in range(4):
                    osort[t * per_tile + g * 4 + j] = out[:, j * HALF : (j + 1) * HALF]

    def both(i, now, later, peaks, running):
        next_peaks, next_running = (), ()
        for g in range(groups):
            next_peaks += score(i + 1, later, (g,))
            next_running += absorb(i, now, peaks[g : g + 1], running[g : g + 1], (g,))
        finish_tile(i)
        return next_peaks, next_running

    def two(h, carry):
        peaks, running = both(2 * h, sa, sb, *carry)
        return both(2 * h + 1, sb, sa, peaks, running)

    running = tuple(jnp.full((1, QN), NEG, F32) for _ in range(groups))
    steps = tiles * (tiles + 1) // 2
    lax.fori_loop(0, steps // 2, two, (score(0, sa, range(groups)), running))

    def o_send(step, flip):
        y = lax.rem(my_y + step // SIDE, SIDE)
        x = lax.rem(my_x + lax.rem(step, SIDE), SIDE)
        target = agent_at(y, x, lax.rem(core + flip, 2))
        return pltpu.make_async_remote_copy(
            src_ref=ost.at[target], dst_ref=att.at[core, chip],
            send_sem=a_send.at[flip * chips + step], recv_sem=a_recv.at[flip * chips + step],
            device_id={"agent": target}, device_id_type=MESH,
        )

    def o_arrival(step, flip):
        y = lax.rem(my_y + SIDE - step // SIDE, SIDE)
        x = lax.rem(my_x + SIDE - lax.rem(step, SIDE), SIDE)
        other = lax.rem(core + flip, 2)
        return pltpu.make_async_remote_copy(
            src_ref=ost.at[me], dst_ref=att.at[other, y * SIDE + x],
            send_sem=a_send.at[flip * chips + step], recv_sem=a_recv.at[flip * chips + step],
            device_id={"agent": agent_at(y, x, other)}, device_id_type=MESH,
        )

    def unsort(target):
        pair = [osort[rank_ref[2 * target]], osort[rank_ref[2 * target + 1]]]
        ost[target] = jnp.concatenate(pair, axis=1).astype(BF)

    own = pltpu.make_async_copy(ost.at[me], att.at[core, chip], local_sem.at[3])
    unsort(sibling)
    o_send(0, 1).start()
    unsort(me)
    own.start()

    def start(n, _):
        step = chip_step(n)
        y, x = there(step)
        unsort(agent_at(y, x, 0))
        unsort(agent_at(y, x, 1))
        o_send(step, 0).start()
        o_send(step, 1).start()
        return 0

    lax.fori_loop(1, chips, start, 0)
    own.wait()
    o_arrival(0, 1).wait_recv()

    def land(step, _):
        o_arrival(step, 0).wait_recv()
        o_arrival(step, 1).wait_recv()
        return 0

    lax.fori_loop(1, chips, land, 0)

    loads[3].wait()
    wide = 256
    for half in range(2):
        rows = jnp.transpose(att[half].reshape(width, BLK))
        seen = jnp.concatenate(
            [obs_ref[half * HALF : (half + 1) * HALF], obs_ref[BLK + half * HALF : BLK + (half + 1) * HALF]], axis=0
        ).astype(F32)
        for n in range(width // wide):
            cols = slice(n * wide, (n + 1) * wide)
            resid[half * BLK : (half + 1) * BLK, cols] = seen[:, cols] + jnp.dot(
                rows, wo[:, cols], preferred_element_type=F32
            )
    whole = resid[...]
    factor = lax.rsqrt(jnp.mean(whole * whole, axis=1, keepdims=True) + 1e-05)
    hid[...] = (whole * factor * gain_ref[...]).astype(BF)

    per_env = 2 * BLK // envs

    def piece(e):
        quarter = lax.rem(e, 4)
        return pl.ds(pl.multiple_of(quarter // 2 * BLK + e // 4 * HALF + lax.rem(quarter, 2) * per_env, per_env), per_env)

    def z_copy(step):
        other = lax.rem(env + step, envs)
        return pltpu.make_async_remote_copy(
            src_ref=hid.at[piece(other)], dst_ref=hbuf.at[env],
            send_sem=z_send.at[step], recv_sem=z_recv.at[step],
            device_id={"env": other}, device_id_type=MESH,
        )

    def z_arrival(step):
        other = lax.rem(env + envs - step, envs)
        return pltpu.make_async_remote_copy(
            src_ref=hid.at[piece(env)], dst_ref=hbuf.at[other],
            send_sem=z_send.at[step], recv_sem=z_recv.at[step],
            device_id={"env": other}, device_id_type=MESH,
        )

    mine = pltpu.make_async_copy(hid.at[piece(env)], hbuf.at[env], local_sem.at[4])
    mine.start()

    def z_start(n, _):
        z_copy(pick(n, (0,) + RING)).start()
        return 0

    lax.fori_loop(1, envs, z_start, 0)
    mine.wait()

    def z_land(step, _):
        z_arrival(step).wait_recv()
        return 0

    lax.fori_loop(1, envs, z_land, 0)

    loads[4].wait()
    loads[5].wait()
    moved = hbuf[...].reshape(envs * per_env, width)
    hidden_units = whead_ref.shape[1]
    for n in range(hidden_units // wide):
        cols = slice(n * wide, (n + 1) * wide)
        mix[:, :, cols] = jnp.dot(moved, wm[:, cols], preferred_element_type=F32).reshape(envs, per_env, wide)
        part[:, :, cols] = jnp.dot(moved, wg[:, cols], preferred_element_type=F32).reshape(envs, per_env, wide)
    partners = []
    values = []
    for e in range(envs):
        partner = jnp.int32(0)
        for f in range(envs):
            if f != e:
                partner = jnp.where(group_ref[f] == group_ref[e], f, partner)
        partners.append(partner)
        x = mix[e] + 0.5 * (part[e] + part[partner])
        activ = 0.5 * x * (1.0 + lax.erf(x * np.float32(np.sqrt(0.5))))
        values.append(jnp.sum(activ * whead_ref[...], axis=1, keepdims=True).T)
    for e in range(envs):
        val_ref[e : e + 1, :] = values[e]
    excess = ret_ref[...] - val_ref[...]
    rows = lax.broadcasted_iota(jnp.int32, (envs, per_env), 0)
    for e in range(envs):
        mine_ = excess[e : e + 1]
        other = jnp.sum(jnp.where(rows == jnp.full(rows.shape, partners[e], jnp.int32), excess, 0.0), axis=0, keepdims=True)
        adv_ref[e : e + 1, :] = mine_ - 0.5 * (mine_ + other)

    own_forward(kst, kbuf, kf_send, kf_recv).wait_send()
    own_forward(vst, vbuf, vf_send, vf_recv).wait_send()
    q_send(0, 1).wait_send()
    o_send(0, 1).wait_send()

    def finish(step, _):
        send(kst, kbuf, ks_send, ks_recv, step).wait_send()
        send(vst, vbuf, vs_send, vs_recv, step).wait_send()
        forward(kbuf, kf_send, kf_recv, step).wait_send()
        forward(vbuf, vf_send, vf_recv, step).wait_send()
        for flip in range(2):
            q_send(step, flip).wait_send()
            o_send(step, flip).wait_send()
        return 0

    lax.fori_loop(1, chips, finish, 0)

    def z_finish(step, _):
        z_copy(step).wait_send()
        return 0

    lax.fori_loop(1, envs, z_finish, 0)


def decoder(rank, group_of_env, visible, obs, actions, table, gain, w_head, returns, w_query, w_key, w_value, w_out, w_mix, w_group):
    rows, width = obs.shape
    envs, per_env = returns.shape
    units = w_head.shape[0]
    blocks = rank.shape[0]
    chips = SIDE * SIDE
    groups = 2
    keys = 4 * groups * BLK
    ids = jnp.arange(blocks, dtype=jnp.int32)
    order = jnp.sum(jnp.where(rank[None, :] == ids[:, None], ids[None, :], 0), axis=1)
    sm = pl.BlockSpec(memory_space=pltpu.SMEM)
    vm = pl.BlockSpec(memory_space=pltpu.VMEM)
    hbm = pl.BlockSpec(memory_space=pl.ANY)
    dma = pltpu.SemaphoreType.DMA
    out = jax.ShapeDtypeStruct((envs, per_env), F32)
    return pl.pallas_call(
        decoder_kernel,
        out_shape=(out, out),
        in_specs=[sm] * 3 + [vm] * 8 + [hbm] * 6,
        out_specs=(vm, vm),
        scratch_shapes=[pltpu.VMEM((width, width), BF)] * 4
        + [pltpu.VMEM((width, units), BF)] * 2
        + [pltpu.VMEM((rows, width), BF)]
        + [pltpu.VMEM((2, width, BLK), BF)] * 3
        + [
            pltpu.VMEM((2 * chips, HD, BLK), BF),
            pltpu.VMEM((blocks, HD, BLK), BF),
            pltpu.VMEM((blocks, HD, BLK), BF),
            pltpu.VMEM((blocks * BLK, HD + blocks), BF),
            pltpu.VMEM((blocks, VROWS, BLK), BF),
            pltpu.VMEM((blocks // 4, HD + blocks, QN), BF),
            pltpu.VMEM((groups, VROWS, QN), F32),
            pltpu.VMEM((blocks, HD, HALF), F32),
            pltpu.VMEM((2 * chips, HD, BLK), BF),
            pltpu.VMEM((groups, keys, QN), F32),
            pltpu.VMEM((groups, keys, QN), F32),
            pltpu.VMEM((2, 2 * BLK, BLK), F32),
            pltpu.VMEM((2, chips, HD, BLK), BF),
            pltpu.VMEM((rows, width), F32),
            pltpu.VMEM((rows, width), BF),
            pltpu.VMEM((envs, per_env, width), BF),
            pltpu.VMEM((envs, per_env, units), F32),
            pltpu.VMEM((envs, per_env, units), F32),
            dma((6,)),
        ]
        + [dma((chips,))] * 4
        + [dma((2 * chips,))] * 2
        + [dma((chips,))] * 4
        + [dma((2 * chips,))] * 2
        + [dma((envs,))] * 2
        + [dma((5,))],
        compiler_params=pltpu.CompilerParams(
            collective_id=0, has_side_effects=True, vmem_limit_bytes=60 * 2**20
        ),
        name="decoder",
    )(
        rank, order, group_of_env, rank[None, :], visible, obs, actions, table, gain[None, :], w_head[None, :], returns,
        w_query, w_key, w_value, w_out, w_mix, w_group,
    )


def on_device(
    obs_rep, actions, action_table, decode_rank, visible, w_query, w_key, w_value, w_out,
    norm_gain, w_mix, w_group, w_head, returns, group_of_env,
):
    return decoder(
        decode_rank, group_of_env, visible, obs_rep[0], actions, action_table, norm_gain, w_head, returns,
        w_query, w_key, w_value, w_out, w_mix, w_group,
    )


def solution(mesh):
    spec = P(None, ("agent", "env"))
    in_specs = (P("env", "agent", None), P("env", "agent")) + (P(),) * 11 + (spec, P())
    return jax.shard_map(
        on_device, mesh=mesh, in_specs=in_specs, out_specs=(spec, spec), check_vma=False
    )
```

time: 99.9 us -> 90.4 us (0.905)
  Pallas kernels: 93.5 us -> 84.4 us
  local copies, waits for them, and re-layouts: 4.88 us -> 2.54 us
  other arithmetic: 0 us -> 1.28 us
    pallas_call x3 -> x1, Pallas kernels: 93.5 us -> 84.4 us  [decoder(): pl.pallas_call(decoder_kernel, out_shape=(out, out), in_specs=[sm] * 3 +...]
    unnamed x32 -> x2, local copies, waits for them, and re-layouts: 4.88 us -> 2.54 us
    reduce_sum x0 -> x1, other arithmetic: none -> 1.28 us  [decoder(): jnp.sum(jnp.where(rank[None, :] == ids[:, None], ids[None, :], 0), axis=1)]
where the time goes in v1:
time: 90.4 us; the launch traced here: 88.8 us
  Pallas kernels  84.4 us (93%)
  local copies, waits for them, and re-layouts  2.54 us (3%)
  other arithmetic  1.28 us (1%)
    pallas_call x1, Pallas kernels, decoder(): pl.pallas_call(decoder_kernel, out_shape=(out, out), in_specs=[sm] * 3 +...  84.4 us
    unnamed x2, local copies, waits for them, and re-layouts  2.54 us

profile of v1, /device:TPU:64, one launch (start us, length us, event | category | flops | bytes accessed | tf_op | source)
XLA Modules:
  0.0 88.8 jit_solution(8941357509820791409)
XLA Ops:
  0.6 1.3 %select_reduce_fusion.order = s32[64]{0:T(128)} fusion(s32[64]{0:T(128)} %rank_ref.1), kind=kLoop, calls=%fused_computation | loop fusion | flops 12224 | bytes 512 | tf_op jit(solution)/shard_map/reduce_sum | solution.py:544
  1.9 84.4 %decoder.1 = (f32[8,32]{1,0:T(8,128)}, f32[8,32]{1,0:T(8,128)}) custom-call(s32[64]{0:T(128)} %rank_ref.1, s32[64]{0:T(128)} %select_reduce_fusion.order, s32[8]{0:T(128)} %group_ref.1, s32[1,64]{1,0:T(1,128)} %bitcast.7, s32[64,64]{1,0:T(8,128)} %visible_ref.1, bf16[256,1024]{1,0:T(8,128)(2,1)} %bitcast.4, s32[1,256]{1,0:T(1,128)} %act_ref.1, ...), custom_call_target="tpu_custom_call" | custom-call | tf_op jit(solution)/shard_map/decoder/pallas_call | solution.py:550
  86.3 1.3 %copy.19 = f32[8,32]{1,0:T(8,128)} copy(f32[8,32]{1,0:T(8,128)} %get-tuple-element.4) | data formatting | bytes 2048
  87.6 1.3 %copy.20 = f32[8,32]{1,0:T(8,128)} copy(f32[8,32]{1,0:T(8,128)} %get-tuple-element.5) | data formatting | bytes 2048

commit v2 on v1

--- a/solution.py
+++ b/solution.py
@@ -28,6 +28,7 @@
     (0, 1), (0, 3), (1, 0), (3, 0), (0, 2), (2, 0), (1, 1), (3, 3),
     (1, 3), (3, 1), (1, 2), (3, 2), (2, 1), (2, 3), (2, 2),
 )
+EARLY = 8
 RING = (1, 7, 2, 6, 3, 5, 4)
 
 
@@ -47,10 +48,10 @@
     wq_hbm, wk_hbm, wv_hbm, wo_hbm, wm_hbm, wg_hbm,
     val_ref, adv_ref,
     wq, wk, wv, wo, wm, wg, tok, kst, vst, qst, qbuf, kbuf, vbuf,
-    ks, vs, qa, acc, osort, ost, sa, sb, mask,
+    ks, vs, qa, acc, osort, ost, sa, sb, pre, pre_peak, mask,
     att, resid, hid, hbuf, mix, part,
     load_sem, ks_send, ks_recv, vs_send, vs_recv, qs_send, qs_recv, kf_send, kf_recv, vf_send, vf_recv,
-    a_send, a_recv, z_send, z_recv, local_sem,
+    a_send, a_recv, z_send, z_recv, local_sem, turn_sem,
 ):
     groups = acc.shape[0]
     env = lax.axis_index("env")
@@ -61,7 +62,7 @@
     my_y, my_x = chip // SIDE, lax.rem(chip, SIDE)
     chips = SIDE * SIDE
     sibling = chip * 2 + 1 - core
-    pairs = ((wk_hbm, wk), (wv_hbm, wv), (wq_hbm, wq), (wo_hbm, wo), (wm_hbm, wm), (wg_hbm, wg))
+    pairs = ((wk_hbm, wk), (wq_hbm, wq), (wv_hbm, wv), (wo_hbm, wo), (wm_hbm, wm), (wg_hbm, wg))
     loads = [pltpu.make_async_copy(src, dst, load_sem.at[n]) for n, (src, dst) in enumerate(pairs)]
     for load in loads[:3]:
         load.start()
@@ -203,13 +204,10 @@
     for load in loads[3:]:
         load.start()
     send_all(kst, kbuf, ks_send, ks_recv, kf_send, kf_recv, 0)
-    loads[1].wait()
-    project(tok[...], wv, vst)
-    send_all(vst, vbuf, vs_send, vs_recv, vf_send, vf_recv, 1)
     rows = jnp.concatenate(
         [obs_ref[0:HALF], obs_ref[BLK : BLK + HALF], obs_ref[HALF:BLK], obs_ref[BLK + HALF :]], axis=0
     )
-    loads[2].wait()
+    loads[1].wait()
     project(rows, wq, qst)
     q_local = pltpu.make_async_copy(qst.at[core, head_rows(my_y, my_x), :], qbuf.at[me], local_sem.at[2])
     q_local.start()
@@ -223,6 +221,9 @@
 
     lax.fori_loop(1, chips, q_one, 0)
 
+    loads[2].wait()
+    project(tok[...], wv, vst)
+    send_all(vst, vbuf, vs_send, vs_recv, vf_send, vf_recv, 1)
     def pass_on(stage, buf, sends, recvs, fsends, frecvs):
         def one(n, _):
             step = chip_step(n)
@@ -300,9 +301,6 @@
     pass_on(kst, kbuf, ks_send, ks_recv, kf_send, kf_recv)
     local(kst, kbuf, 0).wait()
     lax.fori_loop(0, blocks, prepare_keys, 0, unroll=4)
-    pass_on(vst, vbuf, vs_send, vs_recv, vf_send, vf_recv)
-    local(vst, vbuf, 1).wait()
-    lax.fori_loop(0, blocks, prepare_values, 0, unroll=4)
     q_local.wait()
     q_arrival(0, 1).wait_recv()
 
@@ -372,9 +370,29 @@
         peaks, running = both(2 * h, sa, sb, *carry)
         return both(2 * h + 1, sb, sa, peaks, running)
 
+    early = pre.shape[0]
+
+    def score_early(i, _):
+        for g, peak in enumerate(score(i, pre.at[i], range(groups))):
+            pre_peak[i, g : g + 1] = peak
+        return 0
+
+    lax.fori_loop(0, early, score_early, 0)
+    pass_on(vst, vbuf, vs_send, vs_recv, vf_send, vf_recv)
+    local(vst, vbuf, 1).wait()
+    lax.fori_loop(0, blocks, prepare_values, 0, unroll=4)
+
+    def absorb_early(i, running):
+        new = ()
+        for g in range(groups):
+            new += absorb(i, pre.at[i], (pre_peak[i, g : g + 1],), running[g : g + 1], (g,))
+        finish_tile(i)
+        return new
+
     running = tuple(jnp.full((1, QN), NEG, F32) for _ in range(groups))
+    running = lax.fori_loop(0, early, absorb_early, running)
     steps = tiles * (tiles + 1) // 2
-    lax.fori_loop(0, steps // 2, two, (score(0, sa, range(groups)), running))
+    lax.fori_loop(early // 2, steps // 2, two, (score(early, sa, range(groups)), running))
 
     def o_send(step, flip):
         y = lax.rem(my_y + step // SIDE, SIDE)
@@ -401,93 +419,128 @@
         ost[target] = jnp.concatenate(pair, axis=1).astype(BF)
 
     own = pltpu.make_async_copy(ost.at[me], att.at[core, chip], local_sem.at[3])
-    unsort(sibling)
-    o_send(0, 1).start()
-    unsort(me)
-    own.start()
 
     def start(n, _):
         step = chip_step(n)
-        y, x = there(step)
-        unsort(agent_at(y, x, 0))
-        unsort(agent_at(y, x, 1))
         o_send(step, 0).start()
         o_send(step, 1).start()
         return 0
 
-    lax.fori_loop(1, chips, start, 0)
-    own.wait()
-    o_arrival(0, 1).wait_recv()
-
-    def land(step, _):
-        o_arrival(step, 0).wait_recv()
-        o_arrival(step, 1).wait_recv()
-        return 0
-
-    lax.fori_loop(1, chips, land, 0)
-
+    def sent(step, _):
+        o_send(step, 0).wait_send()
+        o_send(step, 1).wait_send()
+        return 0
+
+    def unsort_all(a, _):
+        unsort(a)
+        return 0
+
+    def start_all():
+        o_send(0, 1).start()
+        own.start()
+        lax.fori_loop(1, chips, start, 0)
+
+    def sent_all():
+        o_send(0, 1).wait_send()
+        lax.fori_loop(1, chips, sent, 0)
+
+    lax.fori_loop(0, 2 * chips, unsort_all, 0, unroll=2)
+
+    @pl.when(core == 0)
+    def _():
+        start_all()
+        sent_all()
+        pl.semaphore_signal(turn_sem, inc=1, device_id={"agent": sibling}, device_id_type=MESH)
+
+    @pl.when(core == 1)
+    def _():
+        pl.semaphore_wait(turn_sem, 1)
+        start_all()
+
+    def land_from(which):
+        flip = jnp.where(core == which, 0, 1)
+
+        @pl.when(core == which)
+        def _():
+            own.wait()
+
+        @pl.when(core != which)
+        def _():
+            o_arrival(0, 1).wait_recv()
+
+        def land(step, _):
+            o_arrival(step, flip).wait_recv()
+            return 0
+
+        lax.fori_loop(1, chips, land, 0)
+
+    wide = 256
+    per_env = 2 * BLK // envs
+
+    def piece(e):
+        quarter = lax.rem(e, 4)
+        return pl.ds(pl.multiple_of(quarter // 2 * BLK + e // 4 * HALF + lax.rem(quarter, 2) * per_env, per_env), per_env)
+
+    def z_copy(step):
+        other = lax.rem(env + step, envs)
+        return pltpu.make_async_remote_copy(
+            src_ref=hid.at[piece(other)], dst_ref=hbuf.at[env],
+            send_sem=z_send.at[step], recv_sem=z_recv.at[step],
+            device_id={"env": other}, device_id_type=MESH,
+        )
+
+    def z_arrival(step):
+        other = lax.rem(env + envs - step, envs)
+        return pltpu.make_async_remote_copy(
+            src_ref=hid.at[piece(env)], dst_ref=hbuf.at[other],
+            send_sem=z_send.at[step], recv_sem=z_recv.at[step],
+            device_id={"env": other}, device_id_type=MESH,
+        )
+
+    mine = pltpu.make_async_copy(hid.at[piece(env)], hbuf.at[env], local_sem.at[4])
     loads[3].wait()
-    wide = 256
     for half in range(2):
-        rows = jnp.transpose(att[half].reshape(width, BLK))
+        land_from(half)
+        turned = jnp.transpose(att[half].reshape(width, BLK))
         seen = jnp.concatenate(
             [obs_ref[half * HALF : (half + 1) * HALF], obs_ref[BLK + half * HALF : BLK + (half + 1) * HALF]], axis=0
         ).astype(F32)
         for n in range(width // wide):
             cols = slice(n * wide, (n + 1) * wide)
             resid[half * BLK : (half + 1) * BLK, cols] = seen[:, cols] + jnp.dot(
-                rows, wo[:, cols], preferred_element_type=F32
+                turned, wo[:, cols], preferred_element_type=F32
             )
-    whole = resid[...]
-    factor = lax.rsqrt(jnp.mean(whole * whole, axis=1, keepdims=True) + 1e-05)
-    hid[...] = (whole * factor * gain_ref[...]).astype(BF)
-
-    per_env = 2 * BLK // envs
-
-    def piece(e):
-        quarter = lax.rem(e, 4)
-        return pl.ds(pl.multiple_of(quarter // 2 * BLK + e // 4 * HALF + lax.rem(quarter, 2) * per_env, per_env), per_env)
-
-    def z_copy(step):
-        other = lax.rem(env + step, envs)
-        return pltpu.make_async_remote_copy(
-            src_ref=hid.at[piece(other)], dst_ref=hbuf.at[env],
-            send_sem=z_send.at[step], recv_sem=z_recv.at[step],
-            device_id={"env": other}, device_id_type=MESH,
-        )
-
-    def z_arrival(step):
-        other = lax.rem(env + envs - step, envs)
-        return pltpu.make_async_remote_copy(
-            src_ref=hid.at[piece(env)], dst_ref=hbuf.at[other],
-            send_sem=z_send.at[step], recv_sem=z_recv.at[step],
-            device_id={"env": other}, device_id_type=MESH,
-        )
-
-    mine = pltpu.make_async_copy(hid.at[piece(env)], hbuf.at[env], local_sem.at[4])
+        whole = resid[half * BLK : (half + 1) * BLK, :]
+        factor = lax.rsqrt(jnp.mean(whole * whole, axis=1, keepdims=True) + 1e-05)
+        hid[half * BLK : (half + 1) * BLK, :] = (whole * factor * gain_ref[...]).astype(BF)
+
+        def z_start(n, _):
+            step = pick(n, (0,) + RING)
+
+            @pl.when(lax.rem(lax.rem(env + step, envs), 4) // 2 == half)
+            def _():
+                z_copy(step).start()
+
+            return 0
+
+        lax.fori_loop(1, envs, z_start, 0)
     mine.start()
-
-    def z_start(n, _):
-        z_copy(pick(n, (0,) + RING)).start()
-        return 0
-
-    lax.fori_loop(1, envs, z_start, 0)
-    mine.wait()
-
-    def z_land(step, _):
-        z_arrival(step).wait_recv()
-        return 0
-
-    lax.fori_loop(1, envs, z_land, 0)
-
     loads[4].wait()
     loads[5].wait()
-    moved = hbuf[...].reshape(envs * per_env, width)
-    hidden_units = whead_ref.shape[1]
-    for n in range(hidden_units // wide):
-        cols = slice(n * wide, (n + 1) * wide)
-        mix[:, :, cols] = jnp.dot(moved, wm[:, cols], preferred_element_type=F32).reshape(envs, per_env, wide)
-        part[:, :, cols] = jnp.dot(moved, wg[:, cols], preferred_element_type=F32).reshape(envs, per_env, wide)
+    mine.wait()
+    for together in ((0, 1, 7), (2, 6), (3, 5, 4)):
+        for step in together:
+            if step:
+                z_arrival(step).wait_recv()
+        places = [lax.rem(env + envs - step, envs) for step in together]
+        moved = jnp.concatenate([hbuf[at] for at in places], axis=0)
+        for n in range(whead_ref.shape[1] // wide):
+            cols = slice(n * wide, (n + 1) * wide)
+            mixed = jnp.dot(moved, wm[:, cols], preferred_element_type=F32)
+            parted = jnp.dot(moved, wg[:, cols], preferred_element_type=F32)
+            for m, at in enumerate(places):
+                mix[at, :, cols] = mixed[m * per_env : (m + 1) * per_env]
+                part[at, :, cols] = parted[m * per_env : (m + 1) * per_env]
     partners = []
     values = []
     for e in range(envs):
@@ -511,7 +564,10 @@
     own_forward(kst, kbuf, kf_send, kf_recv).wait_send()
     own_forward(vst, vbuf, vf_send, vf_recv).wait_send()
     q_send(0, 1).wait_send()
-    o_send(0, 1).wait_send()
+
+    @pl.when(core == 1)
+    def _():
+        sent_all()
 
     def finish(step, _):
         send(kst, kbuf, ks_send, ks_recv, step).wait_send()
@@ -520,7 +576,6 @@
         forward(vbuf, vf_send, vf_recv, step).wait_send()
         for flip in range(2):
             q_send(step, flip).wait_send()
-            o_send(step, flip).wait_send()
         return 0
 
     lax.fori_loop(1, chips, finish, 0)
@@ -568,6 +623,8 @@
             pltpu.VMEM((2 * chips, HD, BLK), BF),
             pltpu.VMEM((groups, keys, QN), F32),
             pltpu.VMEM((groups, keys, QN), F32),
+            pltpu.VMEM((EARLY, groups, keys, QN), F32),
+            pltpu.VMEM((EARLY, 8, QN), F32),
             pltpu.VMEM((2, 2 * BLK, BLK), F32),
             pltpu.VMEM((2, chips, HD, BLK), BF),
             pltpu.VMEM((rows, width), F32),
@@ -582,7 +639,7 @@
         + [dma((chips,))] * 4
         + [dma((2 * chips,))] * 2
         + [dma((envs,))] * 2
-        + [dma((5,))],
+        + [dma((5,)), pltpu.SemaphoreType.REGULAR],
         compiler_params=pltpu.CompilerParams(
             collective_id=0, has_side_effects=True, vmem_limit_bytes=60 * 2**20
         ),

time: 90.4 us -> 87.3 us (0.966); the launches traced: 88.8 us -> 87.1 us
  Pallas kernels: 84.4 us -> 82.7 us
    pallas_call x1, Pallas kernels: 84.4 us -> 82.7 us  [decoder(): pl.pallas_call(decoder_kernel, out_shape=(out, out), in_specs=[sm] * 3 +...]
where the time goes in v2:
time: 87.3 us; the launch traced here: 87.1 us
  Pallas kernels  82.7 us (95%)
  local copies, waits for them, and re-layouts  2.54 us (3%)
  other arithmetic  1.28 us (1%)
    pallas_call x1, Pallas kernels, decoder(): pl.pallas_call(decoder_kernel, out_shape=(out, out), in_specs=[sm] * 3 +...  82.7 us
    unnamed x2, local copies, waits for them, and re-layouts  2.54 us

profile of v2, /device:TPU:64, one launch (start us, length us, event | category | flops | bytes accessed | tf_op | source)
XLA Modules:
  0.0 87.1 jit_solution(13009845880711976349)
XLA Ops:
  0.6 1.3 %select_reduce_fusion.order = s32[64]{0:T(128)} fusion(s32[64]{0:T(128)} %rank_ref.1), kind=kLoop, calls=%fused_computation | loop fusion | flops 12224 | bytes 512 | tf_op jit(solution)/shard_map/reduce_sum | solution.py:599
  1.9 82.7 %decoder.1 = (f32[8,32]{1,0:T(8,128)}, f32[8,32]{1,0:T(8,128)}) custom-call(s32[64]{0:T(128)} %rank_ref.1, s32[64]{0:T(128)} %select_reduce_fusion.order, s32[8]{0:T(128)} %group_ref.1, s32[1,64]{1,0:T(1,128)} %bitcast.7, s32[64,64]{1,0:T(8,128)} %visible_ref.1, bf16[256,1024]{1,0:T(8,128)(2,1)} %bitcast.4, s32[1,256]{1,0:T(1,128)} %act_ref.1, ...), custom_call_target="tpu_custom_call" | custom-call | tf_op jit(solution)/shard_map/decoder/pallas_call | solution.py:605
  84.6 1.3 %copy.19 = f32[8,32]{1,0:T(8,128)} copy(f32[8,32]{1,0:T(8,128)} %get-tuple-element.4) | data formatting | bytes 2048
  85.9 1.3 %copy.20 = f32[8,32]{1,0:T(8,128)} copy(f32[8,32]{1,0:T(8,128)} %get-tuple-element.5) | data formatting | bytes 2048

commit v3 on v2

--- a/solution.py
+++ b/solution.py
@@ -44,10 +44,10 @@
 
 
 def decoder_kernel(
-    rank_ref, order, group_ref, rank_row, visible_ref, obs_ref, act_ref, table_ref, gain_ref, whead_ref, ret_ref,
-    wq_hbm, wk_hbm, wv_hbm, wo_hbm, wm_hbm, wg_hbm,
+    rank_ref, order, group_ref, rank_row, visible_ref, act_ref, table_ref, gain_ref, whead_ref, ret_ref,
+    obs_hbm, wq_hbm, wk_hbm, wv_hbm, wo_hbm, wm_hbm, wg_hbm,
     val_ref, adv_ref,
-    wq, wk, wv, wo, wm, wg, tok, kst, vst, qst, qbuf, kbuf, vbuf,
+    obs_ref, wq, wk, wv, wo, wm, wg, tok, kst, vst, qst, qbuf, kbuf, vbuf,
     ks, vs, qa, acc, osort, ost, sa, sb, pre, pre_peak, mask,
     att, resid, hid, hbuf, mix, part,
     load_sem, ks_send, ks_recv, vs_send, vs_recv, qs_send, qs_recv, kf_send, kf_recv, vf_send, vf_recv,
@@ -62,6 +62,8 @@
     my_y, my_x = chip // SIDE, lax.rem(chip, SIDE)
     chips = SIDE * SIDE
     sibling = chip * 2 + 1 - core
+    obs_load = pltpu.make_async_copy(obs_hbm, obs_ref, local_sem.at[5])
+    obs_load.start()
     pairs = ((wk_hbm, wk), (wq_hbm, wq), (wv_hbm, wv), (wo_hbm, wo), (wm_hbm, wm), (wg_hbm, wg))
     loads = [pltpu.make_async_copy(src, dst, load_sem.at[n]) for n, (src, dst) in enumerate(pairs)]
     for load in loads[:3]:
@@ -97,6 +99,7 @@
         tok[:, cols] = (obs_ref[:, cols].astype(F32) + added).astype(BF)
         return 0
 
+    obs_load.wait()
     lax.fori_loop(0, width // strip, embed, 0)
 
     def project(rows, w, out):
@@ -444,16 +447,28 @@
         o_send(0, 1).wait_send()
         lax.fori_loop(1, chips, sent, 0)
 
-    lax.fori_loop(0, 2 * chips, unsort_all, 0, unroll=2)
+    def place_and_start(n, _):
+        step = chip_step(n)
+        y, x = there(step)
+        unsort(agent_at(y, x, 0))
+        unsort(agent_at(y, x, 1))
+        o_send(step, 0).start()
+        o_send(step, 1).start()
+        return 0
 
     @pl.when(core == 0)
     def _():
-        start_all()
+        lax.fori_loop(1, chips, place_and_start, 0)
+        unsort(sibling)
+        unsort(me)
+        o_send(0, 1).start()
+        own.start()
         sent_all()
         pl.semaphore_signal(turn_sem, inc=1, device_id={"agent": sibling}, device_id_type=MESH)
 
     @pl.when(core == 1)
     def _():
+        lax.fori_loop(0, 2 * chips, unsort_all, 0, unroll=2)
         pl.semaphore_wait(turn_sem, 1)
         start_all()
 
@@ -525,6 +540,25 @@
 
         lax.fori_loop(1, envs, z_start, 0)
     mine.start()
+    own_forward(kst, kbuf, kf_send, kf_recv).wait_send()
+    own_forward(vst, vbuf, vf_send, vf_recv).wait_send()
+    q_send(0, 1).wait_send()
+
+    @pl.when(core == 1)
+    def _():
+        sent_all()
+
+    def finish(step, _):
+        send(kst, kbuf, ks_send, ks_recv, step).wait_send()
+        send(vst, vbuf, vs_send, vs_recv, step).wait_send()
+        forward(kbuf, kf_send, kf_recv, step).wait_send()
+        forward(vbuf, vf_send, vf_recv, step).wait_send()
+        for flip in range(2):
+            q_send(step, flip).wait_send()
+        return 0
+
+    lax.fori_loop(1, chips, finish, 0)
+
     loads[4].wait()
     loads[5].wait()
     mine.wait()
@@ -561,25 +595,6 @@
         other = jnp.sum(jnp.where(rows == jnp.full(rows.shape, partners[e], jnp.int32), excess, 0.0), axis=0, keepdims=True)
         adv_ref[e : e + 1, :] = mine_ - 0.5 * (mine_ + other)
 
-    own_forward(kst, kbuf, kf_send, kf_recv).wait_send()
-    own_forward(vst, vbuf, vf_send, vf_recv).wait_send()
-    q_send(0, 1).wait_send()
-
-    @pl.when(core == 1)
-    def _():
-        sent_all()
-
-    def finish(step, _):
-        send(kst, kbuf, ks_send, ks_recv, step).wait_send()
-        send(vst, vbuf, vs_send, vs_recv, step).wait_send()
-        forward(kbuf, kf_send, kf_recv, step).wait_send()
-        forward(vbuf, vf_send, vf_recv, step).wait_send()
-        for flip in range(2):
-            q_send(step, flip).wait_send()
-        return 0
-
-    lax.fori_loop(1, chips, finish, 0)
-
     def z_finish(step, _):
         z_copy(step).wait_send()
         return 0
@@ -605,9 +620,10 @@
     return pl.pallas_call(
         decoder_kernel,
         out_shape=(out, out),
-        in_specs=[sm] * 3 + [vm] * 8 + [hbm] * 6,
+        in_specs=[sm] * 3 + [vm] * 7 + [hbm] * 7,
         out_specs=(vm, vm),
-        scratch_shapes=[pltpu.VMEM((width, width), BF)] * 4
+        scratch_shapes=[pltpu.VMEM((rows, width), BF)]
+        + [pltpu.VMEM((width, width), BF)] * 4
         + [pltpu.VMEM((width, units), BF)] * 2
         + [pltpu.VMEM((rows, width), BF)]
         + [pltpu.VMEM((2, width, BLK), BF)] * 3
@@ -639,14 +655,14 @@
         + [dma((chips,))] * 4
         + [dma((2 * chips,))] * 2
         + [dma((envs,))] * 2
-        + [dma((5,)), pltpu.SemaphoreType.REGULAR],
+        + [dma((6,)), pltpu.SemaphoreType.REGULAR],
         compiler_params=pltpu.CompilerParams(
             collective_id=0, has_side_effects=True, vmem_limit_bytes=60 * 2**20
         ),
         name="decoder",
     )(
-        rank, order, group_of_env, rank[None, :], visible, obs, actions, table, gain[None, :], w_head[None, :], returns,
-        w_query, w_key, w_value, w_out, w_mix, w_group,
+        rank, order, group_of_env, rank[None, :], visible, actions, table, gain[None, :], w_head[None, :], returns,
+        obs, w_query, w_key, w_value, w_out, w_mix, w_group,
     )
 
 

time: 87.3 us -> 85.5 us (0.979)
  Pallas kernels: 82.7 us -> 80.8 us
    pallas_call x1, Pallas kernels: 82.7 us -> 80.8 us  [decoder(): pl.pallas_call(decoder_kernel, out_shape=(out, out), in_specs=[sm] * 3 +...]
where the time goes in v3:
time: 85.5 us; the launch traced here: 85.2 us
  Pallas kernels  80.8 us (95%)
  local copies, waits for them, and re-layouts  2.54 us (3%)
  other arithmetic  1.28 us (1%)
    pallas_call x1, Pallas kernels, decoder(): pl.pallas_call(decoder_kernel, out_shape=(out, out), in_specs=[sm] * 3 +...  80.8 us
    unnamed x2, local copies, waits for them, and re-layouts  2.54 us

profile of v3, /device:TPU:64, one launch (start us, length us, event | category | flops | bytes accessed | tf_op | source)
XLA Modules:
  0.0 85.2 jit_solution(16571938643170965699)
XLA Ops:
  0.6 1.3 %select_reduce_fusion.order = s32[64]{0:T(128)} fusion(s32[64]{0:T(128)} %rank_ref.1), kind=kLoop, calls=%fused_computation | loop fusion | flops 12224 | bytes 512 | tf_op jit(solution)/shard_map/reduce_sum | solution.py:614
  1.9 80.8 %decoder.1 = (f32[8,32]{1,0:T(8,128)}, f32[8,32]{1,0:T(8,128)}) custom-call(s32[64]{0:T(128)} %rank_ref.1, s32[64]{0:T(128)} %select_reduce_fusion.order, s32[8]{0:T(128)} %group_ref.1, s32[1,64]{1,0:T(1,128)} %bitcast.7, s32[64,64]{1,0:T(8,128)} %visible_ref.1, s32[1,256]{1,0:T(1,128)} %act_ref.1, bf16[32,1024]{1,0:T(8,128)(2,1)} %table_ref.1, ...), custom_call_target="tpu_custom_call" | custom-call | tf_op jit(solution)/shard_map/decoder/pallas_call | solution.py:620
  82.7 1.3 %copy.19 = f32[8,32]{1,0:T(8,128)} copy(f32[8,32]{1,0:T(8,128)} %get-tuple-element.4) | data formatting | bytes 2048
  84.0 1.3 %copy.20 = f32[8,32]{1,0:T(8,128)} copy(f32[8,32]{1,0:T(8,128)} %get-tuple-element.5) | data formatting | bytes 2048

commit v4 on v3

--- a/solution.py
+++ b/solution.py
@@ -44,11 +44,11 @@
 
 
 def decoder_kernel(
-    rank_ref, order, group_ref, rank_row, visible_ref, act_ref, table_ref, gain_ref, whead_ref, ret_ref,
+    rank_ref, group_ref, rank_row, visible_ref, act_ref, table_ref, gain_ref, whead_ref, ret_ref,
     obs_hbm, wq_hbm, wk_hbm, wv_hbm, wo_hbm, wm_hbm, wg_hbm,
     val_ref, adv_ref,
     obs_ref, wq, wk, wv, wo, wm, wg, tok, kst, vst, qst, qbuf, kbuf, vbuf,
-    ks, vs, qa, acc, osort, ost, sa, sb, pre, pre_peak, mask,
+    order, order_vec, ks, vs, qa, acc, osort, ost, sa, sb, pre, pre_peak, mask,
     att, resid, hid, hbuf, mix, part,
     load_sem, ks_send, ks_recv, vs_send, vs_recv, qs_send, qs_recv, kf_send, kf_recv, vf_send, vf_recv,
     a_send, a_recv, z_send, z_recv, local_sem, turn_sem,
@@ -87,6 +87,14 @@
     ids_r = lax.broadcasted_iota(jnp.int32, (blocks, blocks), 0)
     ids_c = lax.broadcasted_iota(jnp.int32, (blocks, blocks), 1)
     to_rank = (ids_r == rank_row[...]).astype(F32)
+    order_vec[...] = jnp.zeros_like(order_vec)
+    order_vec[:, 0:blocks] = jnp.where(ids_r == rank_row[...], ids_c, 0)
+    found = order_vec[...]
+    for reach in (64, 32, 16, 8, 4, 2, 1):
+        found = jnp.maximum(found, pltpu.roll(found, reach, 1))
+    order_vec[...] = found
+    order_load = pltpu.make_async_copy(order_vec, order, local_sem.at[6])
+    order_load.start()
 
     onehot = (act_ref[...] == lax.broadcasted_iota(jnp.int32, (table_ref.shape[0], 2 * BLK), 0)).astype(F32)
     onehot = jnp.transpose(onehot).astype(BF)
@@ -248,11 +256,11 @@
     def prepare_keys(r, _):
         at = pl.multiple_of(r * BLK, BLK)
         hot = jnp.where(lane == r, 1.0, 0.0).astype(BF)
-        ks[pl.ds(at, BLK), :] = jnp.concatenate([jnp.transpose(kbuf[order[r]]), hot], axis=1)
+        ks[pl.ds(at, BLK), :] = jnp.concatenate([jnp.transpose(kbuf[order[r, 0]]), hot], axis=1)
         return 0
 
     def prepare_values(r, _):
-        vs[r] = jnp.concatenate([vbuf[order[r]], ones], axis=0)
+        vs[r] = jnp.concatenate([vbuf[order[r, 0]], ones], axis=0)
         return 0
 
     to_rank = to_rank.astype(BF)
@@ -276,7 +284,7 @@
     spread_c = lax.broadcasted_iota(jnp.int32, (blocks, QN), 1)
 
     def half(r, want):
-        b = order[r]
+        b = order[r, 0]
         x = qbuf[b // 2].astype(F32)
         return jnp.where(jnp.full(x.shape, lax.rem(b, 2), jnp.int32) == want, x, pltpu.roll(x, HALF, 1))
 
@@ -301,6 +309,7 @@
         first = j < p + 1
         return jnp.where(first, p, tiles - 1 - p), jnp.where(first, j, j - p - 1)
 
+    order_load.wait()
     pass_on(kst, kbuf, ks_send, ks_recv, kf_send, kf_recv)
     local(kst, kbuf, 0).wait()
     lax.fori_loop(0, blocks, prepare_keys, 0, unroll=4)
@@ -610,8 +619,6 @@
     chips = SIDE * SIDE
     groups = 2
     keys = 4 * groups * BLK
-    ids = jnp.arange(blocks, dtype=jnp.int32)
-    order = jnp.sum(jnp.where(rank[None, :] == ids[:, None], ids[None, :], 0), axis=1)
     sm = pl.BlockSpec(memory_space=pltpu.SMEM)
     vm = pl.BlockSpec(memory_space=pltpu.VMEM)
     hbm = pl.BlockSpec(memory_space=pl.ANY)
@@ -620,7 +627,7 @@
     return pl.pallas_call(
         decoder_kernel,
         out_shape=(out, out),
-        in_specs=[sm] * 3 + [vm] * 7 + [hbm] * 7,
+        in_specs=[sm] * 2 + [vm] * 7 + [hbm] * 7,
         out_specs=(vm, vm),
         scratch_shapes=[pltpu.VMEM((rows, width), BF)]
         + [pltpu.VMEM((width, width), BF)] * 4
@@ -631,6 +638,8 @@
             pltpu.VMEM((2 * chips, HD, BLK), BF),
             pltpu.VMEM((blocks, HD, BLK), BF),
             pltpu.VMEM((blocks, HD, BLK), BF),
+            pltpu.SMEM((blocks, 128), jnp.int32),
+            pltpu.VMEM((blocks, 128), jnp.int32),
             pltpu.VMEM((blocks * BLK, HD + blocks), BF),
             pltpu.VMEM((blocks, VROWS, BLK), BF),
             pltpu.VMEM((blocks // 4, HD + blocks, QN), BF),
@@ -655,13 +664,13 @@
         + [dma((chips,))] * 4
         + [dma((2 * chips,))] * 2
         + [dma((envs,))] * 2
-        + [dma((6,)), pltpu.SemaphoreType.REGULAR],
+        + [dma((7,)), pltpu.SemaphoreType.REGULAR],
         compiler_params=pltpu.CompilerParams(
             collective_id=0, has_side_effects=True, vmem_limit_bytes=60 * 2**20
         ),
         name="decoder",
     )(
-        rank, order, group_of_env, rank[None, :], visible, actions, table, gain[None, :], w_head[None, :], returns,
+        rank, group_of_env, rank[None, :], visible, actions, table, gain[None, :], w_head[None, :], returns,
         obs, w_query, w_key, w_value, w_out, w_mix, w_group,
     )
 

time: 85.5 us -> 84.5 us (0.988)
  other arithmetic: 1.28 us -> 0 us
    reduce_sum x1 -> x0, other arithmetic: 1.28 us -> none  [decoder(): jnp.sum(jnp.where(rank[None, :] == ids[:, None], ids[None, :], 0), axis=1)]
where the time goes in v4:
time: 84.5 us; the launch traced here: 84.3 us
  Pallas kernels  81.1 us (96%)
  local copies, waits for them, and re-layouts  2.53 us (3%)
    pallas_call x1, Pallas kernels, decoder(): pl.pallas_call(decoder_kernel, out_shape=(out, out), in_specs=[sm] * 2 +...  81.1 us
    unnamed x2, local copies, waits for them, and re-layouts  2.53 us

profile of v4, /device:TPU:64, one launch (start us, length us, event | category | flops | bytes accessed | tf_op | source)
XLA Modules:
  0.0 84.3 jit_solution(6510016925005827340)
XLA Ops:
  0.6 81.1 %decoder.1 = (f32[8,32]{1,0:T(8,128)}, f32[8,32]{1,0:T(8,128)}) custom-call(s32[64]{0:T(128)} %rank_ref.1, s32[8]{0:T(128)} %group_ref.1, s32[1,64]{1,0:T(1,128)} %bitcast.7, s32[64,64]{1,0:T(8,128)} %visible_ref.1, s32[1,256]{1,0:T(1,128)} %act_ref.1, bf16[32,1024]{1,0:T(8,128)(2,1)} %table_ref.1, f32[1,1024]{1,0:T(1,128)} %bitcast.5, f32[1,512]{1,0:T(1,128)} %bitcast.6, ...), custom_call_target="tpu_custom_call" | custom-call | tf_op jit(solution)/shard_map/decoder/pallas_call | solution.py:627
  81.8 1.3 %copy.19 = f32[8,32]{1,0:T(8,128)} copy(f32[8,32]{1,0:T(8,128)} %get-tuple-element.4) | data formatting | bytes 2048
  83.0 1.3 %copy.20 = f32[8,32]{1,0:T(8,128)} copy(f32[8,32]{1,0:T(8,128)} %get-tuple-element.5) | data formatting | bytes 2048
